TPU v7x, 128 devices: a whole 4x4x4 slice. The times are simulated.
128 devices in a mesh: seq: 128 (over z, x, y, core).
Axes of the slice: x: 4, y: 4, z: 4, core: 2. Of those that a mesh axis runs over, the one named last changes fastest.
Arguments:
- tokens: bfloat16 [32768, 1024], P('seq'), may hold values from -6 to 6
- w_in: bfloat16 [1024, 4096], replicated, may hold values from -0.1875 to 0.1875
- w_out: bfloat16 [1024, 1024], replicated, may hold values from -0.1875 to 0.1875
- block_counts: int32 [64], replicated, may hold values from 1 to 16, 256 in all
- tails: int32 [64], replicated, may hold values from 1 to 128
- grad_out: bfloat16 [32768, 1024], P('seq'), may hold values from -6 to 6
Outputs:
- layer_out: bfloat16 [32768, 1024], P('seq')
- grad_tokens: bfloat16 [32768, 1024], P('seq')
- grad_w_in: float32 [4096, 1024], P('seq')
Inputs may be any that keep to these rules, and one draw needn't show every extreme that they name: `block_counts`: the block counts sum to 256; one user has exactly 16 blocks.
All inputs are finite; a program needn't handle non-finite values.
Results may differ from a plain program's by a relative error of at most 0.013.
Values may be sent and summed in bfloat16 or wider, within the bound.
A program may use at most 192 MiB of HBM per device.

v0:
```python
import jax
import jax.numpy as jnp
from jax import lax
from jax.sharding import PartitionSpec as P

HEADS = 8
HD = 128
BLK = 128
MAXB = 16


eps = 1e-05


def from_behind(value, axis, steps):
    count = lax.axis_size(axis)
    first, last = (max(0, -steps), min(count, count - steps))
    return lax.ppermute(value, axis, [(source, source + steps) for source in range(first, last)])


def row_info(rows, counts, tails, block_rows):
    ends = jnp.cumsum(counts) * block_rows
    starts = ends - counts * block_rows
    lengths = (counts - 1) * block_rows + tails
    user = jnp.sum((rows[:, None] >= ends[None, :]).astype(jnp.int32), axis=1)
    pick = user[:, None] == jnp.arange(counts.shape[0], dtype=jnp.int32)[None, :]
    start = jnp.sum(jnp.where(pick, starts[None, :], 0), axis=1)
    length = jnp.sum(jnp.where(pick, lengths[None, :], 0), axis=1)
    valid = (rows >= 0) & (rows - start < length)
    return (user, rows, valid)


def attend(query, keys, values, qinfo, kinfo):
    q_user, q_rows, q_ok = qinfo
    k_user, k_rows, k_ok = kinfo
    qh = query.reshape(query.shape[0], HEADS, HD)
    kh = keys.reshape(keys.shape[0], HEADS, HD)
    vh = values.reshape(values.shape[0], HEADS, HD)
    scores = jnp.einsum("qhd,khd->hqk", qh, kh, preferred_element_type=jnp.float32)
    weights = jax.nn.silu(scores * HD ** (-0.5)) / (MAXB * BLK)
    visible = (q_user[:, None] == k_user[None, :]) & (k_rows[None, :] <= q_rows[:, None])
    visible = visible & q_ok[:, None] & k_ok[None, :]
    weights = jnp.where(visible[None], weights, 0.0).astype(jnp.bfloat16)
    out = jnp.einsum("hqk,khd->qhd", weights, vh, preferred_element_type=jnp.float32)
    return out.reshape(query.shape[0], HEADS * HD)


def stem_norm(xf):
    return xf * lax.rsqrt(jnp.mean(xf * xf, axis=-1, keepdims=True) + eps)


def split_parts(pre):
    width = pre.shape[1] // 4
    hidden = jax.nn.silu(pre)
    return tuple((hidden[:, i * width : (i + 1) * width].astype(jnp.bfloat16) for i in range(4)))


def per_device(tokens, w_in, w_out, block_counts, tails, grad_out):
    count = tokens.shape[0]
    reach = MAXB * BLK // count
    me = lax.axis_index("seq")
    local = jnp.arange(count, dtype=jnp.int32)

    def info_at(offset):
        return row_info((me + offset) * count + local, block_counts, tails, BLK)

    own = info_at(0)
    xf = tokens.astype(jnp.float32)
    normed_f, norm_back = jax.vjp(stem_norm, xf)
    normed = normed_f.astype(jnp.bfloat16)
    pre = jnp.dot(normed, w_in, preferred_element_type=jnp.float32)
    parts, split_back = jax.vjp(split_parts, pre)
    u, v, q, k = parts
    own_kv = jnp.stack([k, v])
    attn = attend(q, k, v, own, own)
    kept = []
    moving = own_kv
    for step in range(1, reach + 1):
        moving = from_behind(moving, "seq", 1)
        kept.append(moving)
        attn = attn + attend(q, moving[0], moving[1], own, info_at(-step))

    def tail_fn(attn, u, xf):
        normed_attn = attn * lax.rsqrt(jnp.mean(attn * attn, axis=-1, keepdims=True) + eps)
        gated = (normed_attn * u).astype(jnp.bfloat16)
        return xf + jnp.dot(gated, w_out, preferred_element_type=jnp.float32)

    out_f, tail_back = jax.vjp(tail_fn, attn, u, xf)
    layer_out = out_f.astype(jnp.bfloat16)
    d_attn, d_u, d_xf = tail_back(grad_out.astype(jnp.float32))
    _, local_back = jax.vjp(lambda qq, kk, vv: attend(qq, kk, vv, own, own), q, k, v)
    dq0, dk0, dv0 = local_back(d_attn)
    d_q = dq0.astype(jnp.float32)
    d_k = dk0.astype(jnp.float32)
    d_v = dv0.astype(jnp.float32)
    far_q = q
    far_grad = d_attn
    for step in range(1, reach + 1):
        earlier = kept[step - 1]
        kinfo = info_at(-step)
        _, q_back = jax.vjp(lambda qq: attend(qq, earlier[0], earlier[1], own, kinfo), q)
        d_q = d_q + q_back(d_attn)[0].astype(jnp.float32)
        far_q = from_behind(far_q, "seq", -1)
        far_grad = from_behind(far_grad.astype(jnp.bfloat16), "seq", -1).astype(far_grad.dtype)
        qinfo = info_at(step)
        _, kv_back = jax.vjp(lambda kk, vv: attend(far_q, kk, vv, qinfo, own), k, v)
        dk_far, dv_far = kv_back(far_grad)
        d_k = d_k + dk_far.astype(jnp.float32)
        d_v = d_v + dv_far.astype(jnp.float32)
    d_pre = split_back(
        (d_u, d_v.astype(jnp.bfloat16), d_q.astype(jnp.bfloat16), d_k.astype(jnp.bfloat16))
    )[0]
    d_pre_b = d_pre.astype(jnp.bfloat16)
    grad_w_in = lax.psum_scatter(
        lax.dot_general(
            d_pre_b, normed, (((0,), (0,)), ((), ())), preferred_element_type=jnp.float32
        ),
        "seq",
        scatter_dimension=0,
        tiled=True,
    )
    d_normed = lax.dot_general(
        d_pre_b, w_in, (((1,), (1,)), ((), ())), preferred_element_type=jnp.float32
    )
    grad_tokens = (d_xf + norm_back(d_normed)[0]).astype(jnp.bfloat16)
    return (layer_out, grad_tokens, grad_w_in)


def solution(mesh):
    in_specs = (P("seq", None), P(), P(), P(), P(), P("seq", None))
    out_specs = (P("seq", None), P("seq", None), P("seq", None))
    return jax.shard_map(
        per_device, mesh=mesh, in_specs=in_specs, out_specs=out_specs, check_vma=False
    )
```

profile of v0, /device:TPU:0, one launch (start us, length us, event | category | flops | bytes accessed | tf_op | source)
XLA Modules:
  0.0 1138.2 jit_solution(2249768550690540177)
XLA Ops:
  8.6 8.0 multiply_convert_fusion
  37.9 2.9 fusion.735
  45.0 5.7 collective-permute-start.1
  50.7 2.9 fusion.727
  57.1 3.0 fusion.736
  65.5 2.9 fusion.737
  72.6 20.3 %collective-permute-start.2 = (bf16[2,256,1024]{2,1,0:T(8,128)(2,1)}, bf16[2,256,1024]{2,1,0:T(8,128)(2,1)}, u32[]{:S(2)}, u32[]{:S(2)}) collective-permute-start(bf16[2,256,1024]{2,1,0:T(8,128)(2,1)} %collective-permute-done.1), channel_id=1, source_target_pairs={{0,1},{1,2},{2,3},{3,4},{4,5},{5,6},{6,7},{7,8},{8,9},{9,10},{10,1... | collective-permute-start | bytes 3145736 | tf_op jit(solution)/shard_map/ppermute | solution.py:18
  92.9 2.8 fusion.728
  99.2 3.0 fusion.738
  107.6 2.9 fusion.739
  116.0 9.0 collective-permute-start.3
  131.9 2.9 fusion.740
  138.1 2.9 fusion.741
  147.2 6.9 collective-permute-start.4
  162.1 7.6 collective-permute-start.5
  178.8 7.4 collective-permute-start.6
  195.3 7.2 collective-permute-start.7
  222.4 3.4 multiply_reduce_fusion
  231.7 3.2 fusion.5
  237.4 5.0 fusion.255
  242.4 4.8 fusion.246
  247.2 4.8 fusion.237
  252.0 4.8 fusion.228
  256.8 4.8 fusion.219
  261.5 4.8 fusion.210
  266.3 5.0 fusion.201
  271.2 4.6 fusion.192
  283.1 4.6 fusion.330
  288.9 3.8 fusion.349
  294.1 4.5 fusion.321
  299.7 3.8 fusion.347
  304.8 4.5 fusion.312
  310.4 3.8 fusion.345
  315.8 4.5 fusion.303
  321.4 3.8 fusion.343
  326.5 4.4 fusion.294
  332.1 3.8 fusion.341
  337.8 4.5 fusion.285
  343.5 3.8 fusion.339
  349.5 4.5 fusion.276
  355.1 3.8 fusion.337
  359.3 4.3 fusion.267
  366.8 3.6 fusion.335
  372.4 3.5 fusion.2
  377.2 8.2 fusion.575
  386.6 2.9 fusion.182
  389.6 5.9 fusion.359
  396.6 734.4 %reduce-scatter.2.cloned.1.call-done = f32[32,1024]{1,0:T(8,128)} async-done(((f32[4096,1024]{1,0:T(8,128)}), f32[32,1024]{1,0:T(8,128)}) %reduce-scatter.2.cloned.1.call-update) | async-done | bytes 131088 | tf_op jit(solution)/shard_map/reduce_scatter | solution.py:114
  (297 shorter events, 158.6 us)
Async XLA Ops:
  7.2 215.2 %copy-start = (bf16[1024,1024]{1,0:T(8,128)(2,1)S(1)}, bf16[1024,1024]{1,0:T(8,128)(2,1)}, u32[]{:S(2)}) copy-start(bf16[1024,1024]{1,0:T(8,128)(2,1)} %param.8) | copy-start | bytes 6291460
  7.2 1123.8 %reduce-scatter.2.cloned.1.call-start = ((), (), s32[]{:S(2)}) async-start(), calls=%async_computation.1 | async-start | bytes 16908288 | tf_op jit(solution)/shard_map/reduce_scatter | solution.py:114
  8.6 8.0 copy-start.60
  8.6 8.0 copy-start.58
  18.4 6.0 copy-start.62
  18.4 7.6 copy-start.63
  19.5 21.3 %collective-permute-start = (bf16[2,256,1024]{2,1,0:T(8,128)(2,1)}, bf16[2,256,1024]{2,1,0:T(8,128)(2,1)}, u32[]{:S(2)}, u32[]{:S(2)}) collective-permute-start(bf16[2,256,1024]{2,1,0:T(8,128)(2,1)} %pad_maximum_fusion), channel_id=1, source_target_pairs={{0,1},{1,2},{2,3},{3,4},{4,5},{5,6},{6,7},{7,8},{8,9},{9,10},{10,1... | collective-permute-start | bytes 3145736 | tf_op jit(solution)/shard_map/ppermute | solution.py:18
  21.7 12.8 %collective-permute-start.9 = (bf16[256,1024]{1,0:T(8,128)(2,1)}, bf16[256,1024]{1,0:T(8,128)(2,1)}, u32[]{:S(2)}, u32[]{:S(2)}) collective-permute-start(bf16[256,1024]{1,0:T(8,128)(2,1)} %get-tuple-element.329), channel_id=1, source_target_pairs={{1,0},{2,1},{3,2},{4,3},{5,4},{6,5},{7,6},{8,7},{9,8},{10,9},{11,1... | collective-permute-start | bytes 1572872 | tf_op jit(solution)/shard_map/ppermute | solution.py:18
  36.6 17.0 %collective-permute-start.11 = (bf16[256,1024]{1,0:T(8,128)(2,1)}, bf16[256,1024]{1,0:T(8,128)(2,1)}, u32[]{:S(2)}, u32[]{:S(2)}) collective-permute-start(bf16[256,1024]{1,0:T(8,128)(2,1)} %collective-permute-done.9), channel_id=1, source_target_pairs={{1,0},{2,1},{3,2},{4,3},{5,4},{6,5},{7,6},{8,7},{9,8},{10,9},{11,1... | collective-permute-start | bytes 1572872 | tf_op jit(solution)/shard_map/ppermute | solution.py:18
  45.0 23.3 %collective-permute-start.1 = (bf16[2,256,1024]{2,1,0:T(8,128)(2,1)}, bf16[2,256,1024]{2,1,0:T(8,128)(2,1)}, u32[]{:S(2)}, u32[]{:S(2)}) collective-permute-start(bf16[2,256,1024]{2,1,0:T(8,128)(2,1)} %collective-permute-done), channel_id=1, source_target_pairs={{0,1},{1,2},{2,3},{3,4},{4,5},{5,6},{6,7},{7,8},{8,9},{9,10},{10,1... | collective-permute-start | bytes 3145736 | tf_op jit(solution)/shard_map/ppermute | solution.py:18
  55.7 6.5 collective-permute-start.13
  64.2 31.6 %collective-permute-start.15 = (bf16[256,1024]{1,0:T(8,128)(2,1)}, bf16[256,1024]{1,0:T(8,128)(2,1)}, u32[]{:S(2)}, u32[]{:S(2)}) collective-permute-start(bf16[256,1024]{1,0:T(8,128)(2,1)} %collective-permute-done.13), channel_id=1, source_target_pairs={{1,0},{2,1},{3,2},{4,3},{5,4},{6,5},{7,6},{8,7},{9,8},{10,9},{11,1... | collective-permute-start | bytes 1572872 | tf_op jit(solution)/shard_map/ppermute | solution.py:18
  72.6 37.9 %collective-permute-start.2 = (bf16[2,256,1024]{2,1,0:T(8,128)(2,1)}, bf16[2,256,1024]{2,1,0:T(8,128)(2,1)}, u32[]{:S(2)}, u32[]{:S(2)}) collective-permute-start(bf16[2,256,1024]{2,1,0:T(8,128)(2,1)} %collective-permute-done.1), channel_id=1, source_target_pairs={{0,1},{1,2},{2,3},{3,4},{4,5},{5,6},{6,7},{7,8},{8,9},{9,10},{10,1... | collective-permute-start | bytes 3145736 | tf_op jit(solution)/shard_map/ppermute | solution.py:18
  97.8 6.4 collective-permute-start.17
  106.3 20.3 %collective-permute-start.19 = (bf16[256,1024]{1,0:T(8,128)(2,1)}, bf16[256,1024]{1,0:T(8,128)(2,1)}, u32[]{:S(2)}, u32[]{:S(2)}) collective-permute-start(bf16[256,1024]{1,0:T(8,128)(2,1)} %collective-permute-done.17), channel_id=1, source_target_pairs={{1,0},{2,1},{3,2},{4,3},{5,4},{6,5},{7,6},{8,7},{9,8},{10,9},{11,1... | collective-permute-start | bytes 1572872 | tf_op jit(solution)/shard_map/ppermute | solution.py:18
  114.7 13.2 %copy-start.55 = (pred[256,256]{1,0:T(8,128)(4,1)S(1)}, pred[256,256]{1,0:T(8,128)(4,1)}, u32[]{:S(2)}) copy-start(pred[256,256]{1,0:T(8,128)(4,1)} %get-tuple-element.364) | copy-start | bytes 196612
  114.7 13.2 %copy-start.66 = (f32[8,128,256]{2,1,0:T(8,128)S(1)}, f32[8,128,256]{2,1,0:T(8,128)}, u32[]{:S(2)}) copy-start(f32[8,128,256]{2,1,0:T(8,128)} %convolution_add_fusion.6) | copy-start | bytes 3145732
  116.0 11.9 %copy-start.39 = (bf16[32,8,8,128]{3,2,1,0:T(8,128)(2,1)}, bf16[32,8,8,128]{3,2,1,0:T(8,128)(2,1)S(1)}, u32[]{:S(2)}) copy-start(bf16[32,8,8,128]{3,2,1,0:T(8,128)(2,1)S(1)} %copy.403) | copy-start | bytes 1572868
  116.0 25.0 %collective-permute-start.3 = (bf16[2,256,1024]{2,1,0:T(8,128)(2,1)}, bf16[2,256,1024]{2,1,0:T(8,128)(2,1)}, u32[]{:S(2)}, u32[]{:S(2)}) collective-permute-start(bf16[2,256,1024]{2,1,0:T(8,128)(2,1)} %collective-permute-done.2), channel_id=1, source_target_pairs={{0,1},{1,2},{2,3},{3,4},{4,5},{5,6},{6,7},{7,8},{8,9},{9,10},{10,1... | collective-permute-start | bytes 3145736 | tf_op jit(solution)/shard_map/ppermute | solution.py:18
  126.6 8.2 collective-permute-start.21
  136.8 17.2 %collective-permute-start.23 = (bf16[256,1024]{1,0:T(8,128)(2,1)}, bf16[256,1024]{1,0:T(8,128)(2,1)}, u32[]{:S(2)}, u32[]{:S(2)}) collective-permute-start(bf16[256,1024]{1,0:T(8,128)(2,1)} %collective-permute-done.21), channel_id=1, source_target_pairs={{1,0},{2,1},{3,2},{4,3},{5,4},{6,5},{7,6},{8,7},{9,8},{10,9},{11,1... | collective-permute-start | bytes 1572872 | tf_op jit(solution)/shard_map/ppermute | solution.py:18
  147.2 15.0 %collective-permute-start.4 = (bf16[2,256,1024]{2,1,0:T(8,128)(2,1)}, bf16[2,256,1024]{2,1,0:T(8,128)(2,1)}, u32[]{:S(2)}, u32[]{:S(2)}) collective-permute-start(bf16[2,256,1024]{2,1,0:T(8,128)(2,1)} %collective-permute-done.3), channel_id=1, source_target_pairs={{0,1},{1,2},{2,3},{3,4},{4,5},{5,6},{6,7},{7,8},{8,9},{9,10},{10,1... | collective-permute-start | bytes 3145736 | tf_op jit(solution)/shard_map/ppermute | solution.py:18
  162.1 16.7 %collective-permute-start.5 = (bf16[2,256,1024]{2,1,0:T(8,128)(2,1)}, bf16[2,256,1024]{2,1,0:T(8,128)(2,1)}, u32[]{:S(2)}, u32[]{:S(2)}) collective-permute-start(bf16[2,256,1024]{2,1,0:T(8,128)(2,1)} %collective-permute-done.4), channel_id=1, source_target_pairs={{0,1},{1,2},{2,3},{3,4},{4,5},{5,6},{6,7},{7,8},{8,9},{9,10},{10,1... | collective-permute-start | bytes 3145736 | tf_op jit(solution)/shard_map/ppermute | solution.py:18
  178.8 16.5 %collective-permute-start.6 = (bf16[2,256,1024]{2,1,0:T(8,128)(2,1)}, bf16[2,256,1024]{2,1,0:T(8,128)(2,1)}, u32[]{:S(2)}, u32[]{:S(2)}) collective-permute-start(bf16[2,256,1024]{2,1,0:T(8,128)(2,1)} %collective-permute-done.5), channel_id=1, source_target_pairs={{0,1},{1,2},{2,3},{3,4},{4,5},{5,6},{6,7},{7,8},{8,9},{9,10},{10,1... | collective-permute-start | bytes 3145736 | tf_op jit(solution)/shard_map/ppermute | solution.py:18
  195.3 16.4 %collective-permute-start.7 = (bf16[2,256,1024]{2,1,0:T(8,128)(2,1)}, bf16[2,256,1024]{2,1,0:T(8,128)(2,1)}, u32[]{:S(2)}, u32[]{:S(2)}) collective-permute-start(bf16[2,256,1024]{2,1,0:T(8,128)(2,1)} %collective-permute-done.6), channel_id=1, source_target_pairs={{0,1},{1,2},{2,3},{3,4},{4,5},{5,6},{6,7},{7,8},{8,9},{9,10},{10,1... | collective-permute-start | bytes 3145736 | tf_op jit(solution)/shard_map/ppermute | solution.py:18
  230.0 51.8 %collective-permute-start.8 = (bf16[256,1024]{1,0:T(8,128)(2,1)}, bf16[256,1024]{1,0:T(8,128)(2,1)}, u32[]{:S(2)}, u32[]{:S(2)}) collective-permute-start(bf16[256,1024]{1,0:T(8,128)(2,1)} %add_add_fusion.1), channel_id=1, source_target_pairs={{1,0},{2,1},{3,2},{4,3},{5,4},{6,5},{7,6},{8,7},{9,8},{10,9},{11,1... | collective-permute-start | bytes 1572872 | tf_op jit(solution)/shard_map/ppermute | solution.py:18
  277.9 5.2 copy-start.52
  281.8 10.9 collective-permute-start.10
  288.9 5.2 copy-start.24
  288.9 5.2 copy-start.35
  288.9 5.2 copy-start.51
  292.7 10.8 collective-permute-start.12
  303.5 10.7 collective-permute-start.14
  310.4 5.3 copy-start.26
  310.4 5.3 copy-start.49
  314.2 11.0 collective-permute-start.16
  321.4 5.1 copy-start.25
  321.4 5.1 copy-start.48
  325.2 11.3 collective-permute-start.18
  332.1 5.7 copy-start.30
  332.1 5.7 copy-start.46
  336.5 11.4 collective-permute-start.20
  343.4 6.0 copy-start.27
  343.4 6.0 copy-start.47
  347.9 11.4 collective-permute-start.22
  366.7 5.6 copy-start.11
  389.5 5.9 copy-start.61
  389.5 5.9 copy-start.21
  (48 other events, 145.6 us)
Sparse Core Ops, SparseCore 0:
  385.5 745.3 reduce-scatter.1
where the time goes:
time: 1150 us; the launch traced here: 1140 us
  waiting for transfers between devices  736 us (64%)
  matrix products  198 us (17%)
  starting transfers between devices  88 us (8%)
  local copies, waits for them, and re-layouts  86.3 us (8%)
  between operations  15.7 us (1%)
  other arithmetic  14.3 us (1%)
    reduce_scatter x1, waiting for transfers between devices, per_device(): lax.psum_scatter(lax.dot_general(d_pre_b, normed, (((0,), (0,)), ((), ())...  734 us
    dot_general x35, matrix products, attend(): jnp.einsum('qhd,khd->hqk', qh, kh, preferred_element_type=jnp.float32)  118 us
    ppermute x24, starting transfers between devices, from_behind(): lax.ppermute(value, axis, [(source, source + steps) for source in range(f...  88 us
    dot_general x19, matrix products, attend(): jnp.einsum('hqk,khd->qhd', weights, vh, preferred_element_type=jnp.float32)  51.6 us
    unnamed x166, local copies, waits for them, and re-layouts  38.5 us
  transfers between devices with their start and end apart: 25, of which 4 were waited for; matrix products, arithmetic and copies ran while one was open for 21% of the time, Pallas kernels for 0%

commit v1 on v0

v1 whole, which is shorter than its diff:
```python
import functools

import jax
import jax.numpy as jnp
from jax import lax
from jax.experimental import pallas as pl
from jax.experimental.pallas import tpu as pltpu
from jax.sharding import PartitionSpec as P

MESH = pl.DeviceIdType.MESH
HEADS = 8
HD = 128
BLK = 128
TQ = 256
D = 1024
eps = 1e-05
HALF = 0.5 * HD ** (-0.5)
NT = (((1,), (1,)), ((), ()))
NN = (((1,), (0,)), ((), ()))
TN = (((0,), (0,)), ((), ()))


def dot(a, b, dims, precision=None):
    return lax.dot_general(a, b, dims, precision=precision, preferred_element_type=jnp.float32)


def tile_bounds(start_ref, t, own):
    lo_a, lo_b = start_ref[2 * t], start_ref[2 * t + 1]
    diag = own + t
    return lo_a, lo_b, lo_a // 2, jnp.minimum((lo_b + 1) // 2, diag), diag


def row_valid(rows_ref, t):
    at = lax.broadcasted_iota(jnp.int32, (TQ, HD), 0)
    limit = jnp.where(at < BLK, rows_ref[2 * t], rows_ref[2 * t + 1] + BLK)
    return at < limit


def keep_mask(lo_a, lo_b, diag, kt):
    r = lax.broadcasted_iota(jnp.int32, (TQ, TQ), 0)
    c = lax.broadcasted_iota(jnp.int32, (TQ, TQ), 1) + kt * TQ
    lo = jnp.where(r < BLK, lo_a * BLK, lo_b * BLK)
    return (c >= lo) & (c <= r + diag * TQ)


def fwd_kernel(own, start_ref, rows_ref, q_ref, k_ref, v_ref, u_ref, dg_ref, attn_ref, stat_ref):
    tiles = q_ref.shape[0] // TQ

    @pl.loop(0, tiles)
    def _(t):
        at = pl.ds(pl.multiple_of(t * TQ, TQ), TQ)
        q = jnp.where(row_valid(rows_ref, t), q_ref[at, :].astype(jnp.float32) * HALF, 0.0).astype(jnp.bfloat16)
        lo_a, lo_b, first, full, diag = tile_bounds(start_ref, t, own)

        def body(masked, kt, acc):
            cols = pl.ds(pl.multiple_of(kt * TQ, TQ), TQ)
            x = dot(q, k_ref[cols, :], NT)
            if masked:
                x = jnp.where(keep_mask(lo_a, lo_b, diag, kt), x, 0.0)
            w = (x + x * jnp.tanh(x)).astype(jnp.bfloat16)
            return acc + dot(w, v_ref[cols, :], NN)

        acc = lax.fori_loop(first, full, functools.partial(body, True), jnp.zeros((TQ, HD), jnp.float32))
        acc = lax.fori_loop(full, diag, functools.partial(body, False), acc)
        acc = body(True, diag, acc) * (1.0 / 2048)
        attn_ref[at, :] = acc
        ones = jnp.ones((8, HD), jnp.float32)
        da = dg_ref[at, :].astype(jnp.float32) * u_ref[at, :].astype(jnp.float32)
        for s, val in enumerate((acc * acc, da * acc)):
            sums = dot(ones, val, NT)
            stat_ref[s, pl.ds(2 * t, 1), :] = sums[0:1, :BLK]
            stat_ref[s, pl.ds(2 * t + 1, 1), :] = sums[0:1, BLK:]


def column(stat, t):
    tall = []
    for half in range(2):
        pick = lax.broadcasted_iota(jnp.int32, (16, HD), 0) == 2 * t + half
        tall.append(dot(stat, pick.astype(jnp.float32), TN, lax.Precision.HIGHEST))
    return jnp.concatenate(tall, axis=0)


def bwd_kernel(own, start_ref, rows_ref, q_ref, k_ref, v_ref, u_ref, dg_ref, attn_ref, stat_ref,
               gated_ref, du_ref, dq_ref, dk_ref, dv_ref):
    tiles = q_ref.shape[0] // TQ
    dk_ref[...] = jnp.zeros_like(dk_ref)
    dv_ref[...] = jnp.zeros_like(dv_ref)

    @pl.loop(0, tiles)
    def _(t):
        at = pl.ds(pl.multiple_of(t * TQ, TQ), TQ)
        valid = row_valid(rows_ref, t)
        q = jnp.where(valid, q_ref[at, :].astype(jnp.float32) * HALF, 0.0).astype(jnp.bfloat16)
        square = column(stat_ref[0], t)
        cross = column(stat_ref[1], t)
        r = lax.rsqrt(square * (1.0 / D) + eps)
        attn = attn_ref[at, :]
        u = u_ref[at, :].astype(jnp.float32)
        dg = dg_ref[at, :].astype(jnp.float32)
        na = attn * r
        gated_ref[at, :] = (na * u).astype(gated_ref.dtype)
        du_ref[at, :] = (na * dg).astype(du_ref.dtype)
        d_attn = r * (dg * u) - na * (r * r * cross * (1.0 / D))
        do = jnp.where(valid, d_attn, 0.0).astype(jnp.bfloat16)
        lo_a, lo_b, first, full, diag = tile_bounds(start_ref, t, own)

        def body(masked, kt, dq):
            cols = pl.ds(pl.multiple_of(kt * TQ, TQ), TQ)
            k = k_ref[cols, :]
            x = dot(q, k, NT)
            dw = dot(do, v_ref[cols, :], NT)
            a = 1.0 + jnp.tanh(x)
            w = x * a
            ds = dw * (a + w * (2.0 - a))
            if masked:
                keep = keep_mask(lo_a, lo_b, diag, kt)
                w = jnp.where(keep, w, 0.0)
                ds = jnp.where(keep, ds, 0.0)
            w = w.astype(jnp.bfloat16)
            ds = ds.astype(jnp.bfloat16)
            dv_ref[cols, :] += dot(w, do, TN)
            dk_ref[cols, :] += dot(ds, q, TN)
            return dq + dot(ds, k, NN)

        dq = lax.fori_loop(first, full, functools.partial(body, True), jnp.zeros((TQ, HD), jnp.float32))
        dq = lax.fori_loop(full, diag, functools.partial(body, False), dq)
        dq = body(True, diag, dq)
        dq_ref[at, :] = dq * (HALF / 2048)


def remote(src, dst, send, recv, device):
    return pltpu.make_async_remote_copy(
        src_ref=src, dst_ref=dst, send_sem=send, recv_sem=recv, device_id=(device,), device_id_type=MESH
    )


def greet(devices):
    barrier = pltpu.get_barrier_semaphore()
    for device in devices:
        pl.semaphore_signal(barrier, inc=1, device_id=(device,), device_id_type=MESH)
    return barrier


def place():
    me = lax.axis_index("seq")
    return me, lax.rem(me, HEADS), me // HEADS


def group_peers(me, pos):
    return [me - pos + lax.rem(pos + step, HEADS) for step in range(1, HEADS)]


def gather_kernel(x_ref, dg_ref, x_out, dg_out, local, link_s, link_r, core_s, core_r, dg_s, dg_r):
    me, pos, _ = place()
    base, core, y = me - pos, lax.rem(pos, 2), pos // 2
    peers = group_peers(me, pos)
    pl.semaphore_wait(greet(peers), len(peers))
    rows = x_ref.shape[0]
    half = rows // 2
    halves = [pl.ds(0, half), pl.ds(half, half)]

    def at(step):
        return lax.rem(y + step + 4, 4) * 2 + core

    ahead, behind, other = base + at(1), base + at(-1), base + pos + 1 - 2 * core
    own = [
        pltpu.make_async_copy(x_ref, x_out.at[pos], local.at[0]),
        pltpu.make_async_copy(dg_ref.at[:, pl.ds(pl.multiple_of(pos * HD, HD), HD)], dg_out.at[pos], local.at[1]),
    ]
    for copy in own:
        copy.start()
    sent = []

    def send(src, dst, s, r, device):
        copy = remote(src, dst, s, r, device)
        copy.start()
        sent.append(copy)
        return copy

    first = {}
    for h in (0, 1):
        first["up", h] = send(x_ref.at[halves[h]], x_out.at[pos, halves[h]], link_s.at[0, h], link_r.at[0, h], ahead)
        first["down", 1 - h] = send(
            x_ref.at[halves[1 - h]], x_out.at[pos, halves[1 - h]], link_s.at[1, 1 - h], link_r.at[1, 1 - h], behind)
    cores = [send(x_ref, x_out.at[pos], core_s.at[0], core_r.at[0], other)]
    for i, peer in enumerate(peers):
        to = lax.rem(pos + i + 1, HEADS)
        send(dg_ref.at[:, pl.ds(pl.multiple_of(to * HD, HD), HD)], dg_out.at[pos], dg_s.at[i], dg_r.at[i], peer)
    low, high, far = at(-1), at(1), at(2)
    first["up", 0].wait_recv()
    second_up = send(x_out.at[low, halves[0]], x_out.at[low, halves[0]], link_s.at[2, 0], link_r.at[2, 0], ahead)
    first["down", 1].wait_recv()
    second_down = send(x_out.at[high, halves[1]], x_out.at[high, halves[1]], link_s.at[2, 1], link_r.at[2, 1], behind)
    first["up", 1].wait_recv()
    cores.append(send(x_out.at[low], x_out.at[low], core_s.at[1], core_r.at[1], other))
    first["down", 0].wait_recv()
    cores.append(send(x_out.at[high], x_out.at[high], core_s.at[2], core_r.at[2], other))
    second_up.wait_recv()
    second_down.wait_recv()
    cores.append(send(x_out.at[far], x_out.at[far], core_s.at[3], core_r.at[3], other))
    for copy in cores:
        copy.wait_recv()
    for i in range(HEADS - 1):
        sent[5 + i].wait_recv()
    for copy in sent:
        copy.wait_send()
    for copy in own:
        copy.wait()


def gather(x, dg):
    rows = x.shape[0]
    dma = pltpu.SemaphoreType.DMA
    return pl.pallas_call(
        gather_kernel,
        out_shape=[
            jax.ShapeDtypeStruct((HEADS, rows, D), jnp.bfloat16),
            jax.ShapeDtypeStruct((HEADS, rows, HD), jnp.bfloat16),
        ],
        in_specs=[pl.BlockSpec(memory_space=pl.ANY)] * 2,
        out_specs=[pl.BlockSpec(memory_space=pl.ANY)] * 2,
        scratch_shapes=[dma((2,)), dma((3, 2)), dma((3, 2)), dma((4,)), dma((4,)), dma((7,)), dma((7,))],
        compiler_params=pltpu.CompilerParams(collective_id=1, has_side_effects=True),
        name="gather",
    )(x, dg)


def stats_kernel(s_ref, out_ref, held, send_sem, recv_sem):
    me, pos, _ = place()
    peers = group_peers(me, pos)
    pl.semaphore_wait(greet(peers), len(peers))
    copies = []
    for i, peer in enumerate(peers):
        copy = remote(s_ref, held.at[i], send_sem.at[i], recv_sem.at[i], peer)
        copy.start()
        copies.append(copy)
    total = s_ref[...]
    for i, copy in enumerate(copies):
        copy.wait_recv()
        total = total + held[i]
    out_ref[...] = total
    for copy in copies:
        copy.wait_send()


def sum_stats(stats):
    dma = pltpu.SemaphoreType.DMA
    return pl.pallas_call(
        stats_kernel,
        out_shape=jax.ShapeDtypeStruct(stats.shape, jnp.float32),
        in_specs=[pl.BlockSpec(memory_space=pltpu.VMEM)],
        out_specs=pl.BlockSpec(memory_space=pltpu.VMEM),
        scratch_shapes=[pltpu.VMEM((7,) + stats.shape, jnp.float32), dma((7,)), dma((7,))],
        compiler_params=pltpu.CompilerParams(collective_id=2, has_side_effects=True),
        name="stats",
    )(stats)


def final_kernel(d_ref, g_ref, w_ref, d_out, g_out, w_out, held, total, local, d_s, d_r, g_s, g_r, w_s, w_r, last_s, last_r):
    me, pos, group = place()
    base = me - pos
    groups = held.shape[0]
    rows = d_out.shape[0]
    piece = held.shape[1]
    peers = group_peers(me, pos)
    plane = [lax.rem(group + step, groups) * HEADS + pos for step in range(1, groups)]
    dest = (group // 4) * 32 + pos * 4 + lax.rem(group, 4)
    source = ((me // 32) * 4 + lax.rem(me, 4)) * HEADS + lax.rem(me, 32) // 4
    barrier = greet(peers + plane)

    @pl.when(source != me)
    def _():
        pl.semaphore_signal(barrier, inc=1, device_id=(source,), device_id_type=MESH)

    pl.semaphore_wait(barrier, len(peers) + len(plane) + jnp.where(dest != me, 1, 0))

    def part(p):
        return pl.ds(pl.multiple_of(p * piece, piece), piece)

    keep = pltpu.make_async_copy(w_ref.at[part(group)], held.at[group], local.at[0])
    keep.start()
    scattered = []
    for i, peer in enumerate(plane):
        to = lax.rem(group + i + 1, groups)
        copy = remote(w_ref.at[part(to)], held.at[group], w_s.at[i], w_r.at[i], peer)
        copy.start()
        scattered.append(copy)
    mine = pl.ds(pl.multiple_of(pos * HD, HD), HD)
    moved, own = [], []

    def block(p):
        return pl.ds(pl.multiple_of(p * rows, rows), rows)

    for b in range(4):
        cols = pl.ds(pl.multiple_of(b * D + pos * HD, HD), HD)
        own.append(pltpu.make_async_copy(d_ref.at[b, block(pos)], d_out.at[:, cols], local.at[1 + b]))
    own.append(pltpu.make_async_copy(g_ref.at[block(pos)], g_out.at[:, mine], local.at[5]))
    for copy in own:
        copy.start()
    for i, peer in enumerate(peers):
        to = lax.rem(pos + i + 1, HEADS)
        for b in range(4):
            cols = pl.ds(pl.multiple_of(b * D + pos * HD, HD), HD)
            moved.append(remote(d_ref.at[b, block(to)], d_out.at[:, cols], d_s.at[b, i], d_r.at[b, i], peer))
        moved.append(remote(g_ref.at[block(to)], g_out.at[:, mine], g_s.at[i], g_r.at[i], peer))
    for copy in moved:
        copy.start()
    keep.wait()
    for copy in scattered:
        copy.wait_recv()
    acc = held[0].astype(jnp.float32)
    for g in range(1, groups):
        acc = acc + held[g].astype(jnp.float32)
    total[...] = acc

    @pl.when(dest != me)
    def _():
        copy = remote(total, w_out, last_s, last_r, dest)
        copy.start()
        copy.wait()

    @pl.when(dest == me)
    def _():
        copy = pltpu.make_async_copy(total, w_out, local.at[0])
        copy.start()
        copy.wait()

    for copy in moved:
        copy.wait_recv()
    for copy in moved + scattered:
        copy.wait_send()
    for copy in own:
        copy.wait()


def final(d_pre, gated, gw, groups, rows):
    dma = pltpu.SemaphoreType.DMA
    piece = gw.shape[0] // groups
    anywhere = pl.BlockSpec(memory_space=pl.ANY)
    return pl.pallas_call(
        final_kernel,
        out_shape=[
            jax.ShapeDtypeStruct((rows, 4 * D), jnp.bfloat16),
            jax.ShapeDtypeStruct((rows, D), jnp.bfloat16),
            jax.ShapeDtypeStruct((piece, D), jnp.float32),
        ],
        in_specs=[anywhere] * 3,
        out_specs=[anywhere] * 3,
        scratch_shapes=[
            pltpu.VMEM((groups, piece, D), jnp.bfloat16),
            pltpu.VMEM((piece, D), jnp.float32),
            dma((6,)), dma((4, 7)), dma((4, 7)), dma((7,)), dma((7,)),
            dma((groups - 1,)), dma((groups - 1,)), dma(()), dma(()),
        ],
        compiler_params=pltpu.CompilerParams(collective_id=3, has_side_effects=True),
        name="final",
    )(d_pre, gated, gw)


def block_tables(counts, tails, group, own):
    n = counts.shape[0]
    order = jnp.arange(n, dtype=jnp.int32)
    ends = jnp.sum(jnp.where(order[None, :] <= order[:, None], counts[None, :], 0), axis=1)
    blocks = group * own + jnp.arange(own, dtype=jnp.int32)
    starts = ends - counts
    start = jnp.max(jnp.where(starts[None, :] <= blocks[:, None], starts[None, :], 0), axis=1)
    short = jnp.sum(jnp.where(ends[None, :] - 1 == blocks[:, None], tails[None, :] - BLK, 0), axis=1)
    return start - (group - 1) * own, short + BLK


def attention_call(kernel, name, tables, arrays, outs, flops):
    vmem = pl.BlockSpec(memory_space=pltpu.VMEM)
    return pl.pallas_call(
        kernel,
        grid_spec=pltpu.PrefetchScalarGridSpec(
            num_scalar_prefetch=2, grid=(1,), in_specs=[vmem] * len(arrays), out_specs=[vmem] * len(outs)),
        out_shape=outs,
        compiler_params=pltpu.CompilerParams(vmem_limit_bytes=40 * 2**20),
        cost_estimate=pl.CostEstimate(flops=flops, bytes_accessed=4 * 2**20, transcendentals=2**21),
        name=name,
    )(*tables, *arrays)


def per_device(n, tokens, w_in, w_out, counts, tails, grad_out):
    rows = tokens.shape[0]
    span = rows * HEADS
    groups = n // HEADS
    me, pos, group = place()
    tables = block_tables(counts, tails, group, span // BLK)
    shape = jax.ShapeDtypeStruct
    bf, f32 = jnp.bfloat16, jnp.float32
    xf = tokens.astype(f32)
    inv = lax.rsqrt(jnp.mean(xf * xf, axis=-1, keepdims=True) + eps)
    normed = (xf * inv).astype(bf)
    d_gated = dot(grad_out, w_out, NT).astype(bf)
    all_normed, dg = gather(normed, d_gated)
    all_normed = all_normed.reshape(span, D)
    dg = dg.reshape(span, HD)
    w_head = lax.dynamic_slice(w_in.reshape(D, 4, D), (0, 0, pos * HD), (D, 4, HD)).reshape(D, 4 * HD)
    pre = dot(all_normed, w_head, NN)
    sig = jax.nn.sigmoid(pre)
    hidden = (pre * sig).astype(bf)
    slope = (sig * (1.0 + pre * (1.0 - sig))).astype(bf)
    u, v, q, k = (hidden[:, i * HD : (i + 1) * HD] for i in range(4))
    forward = [(i, i + HEADS) for i in range(n - HEADS)]
    behind = lax.ppermute(jnp.stack([k, v]), "seq", forward)
    k_all = jnp.concatenate([behind[0], k])
    v_all = jnp.concatenate([behind[1], v])
    own = span // TQ
    stat_shape = (2, span // BLK, HD)
    attn, stats = attention_call(
        functools.partial(fwd_kernel, own), "attn_fwd", tables, (q, k_all, v_all, u, dg),
        [shape((span, HD), f32), shape(stat_shape, f32)], 10**9)
    stats = sum_stats(stats)
    gated, d_u, d_q, d_k, d_v = attention_call(
        functools.partial(bwd_kernel, own), "attn_bwd", tables, (q, k_all, v_all, u, dg, attn, stats),
        [shape((span, HD), bf), shape((span, HD), bf), shape((span, HD), f32),
         shape((2 * span, HD), f32), shape((2 * span, HD), f32)], 2 * 10**9)
    far = jnp.stack([d_k[:span], d_v[:span]]).astype(bf)
    ahead = lax.ppermute(far, "seq", [(i + HEADS, i) for i in range(n - HEADS)]).astype(f32)
    d_k = (d_k[span:] + ahead[0]) * (1.0 / 2048)
    d_v = (d_v[span:] + ahead[1]) * (1.0 / 2048)
    d_pre = jnp.stack([
        (d.astype(f32) * slope[:, i * HD : (i + 1) * HD].astype(f32)).astype(bf)
        for i, d in enumerate((d_u, d_v, d_q, d_k))
    ])
    gw = jnp.concatenate([dot(d_pre[i], all_normed, TN).astype(bf) for i in range(4)])
    d_full, g_full, grad_w = final(d_pre, gated, gw, groups, rows)
    gf = grad_out.astype(f32)
    layer_out = (xf + dot(g_full, w_out, NN)).astype(bf)
    d_normed = dot(d_full, w_in, NT)
    mean = jnp.mean(d_normed * xf, axis=-1, keepdims=True)
    grad_tokens = (gf + inv * (d_normed - xf * (inv * inv * mean))).astype(bf)
    return layer_out, grad_tokens, grad_w


def solution(mesh):
    in_specs = (P("seq", None), P(), P(), P(), P(), P("seq", None))
    out_specs = (P("seq", None), P("seq", None), P("seq", None))
    return jax.shard_map(
        functools.partial(per_device, mesh.shape["seq"]),
        mesh=mesh, in_specs=in_specs, out_specs=out_specs, check_vma=False,
    )
```

time: 1150 us -> 233 us (0.20)
  the two profiles are of different devices: /device:TPU:0 before, /device:TPU:15 now
where the time goes in v1:
time: 233 us; the launch traced here: 232 us
  Pallas kernels  118 us (51%)
  waiting for transfers between devices  47.6 us (20%)
  local copies, waits for them, and re-layouts  28.2 us (12%)
  matrix products  20.6 us (9%)
  other arithmetic  10.9 us (5%)
  starting transfers between devices  5.68 us (2%)
    pallas_call x1, Pallas kernels, final(): pl.pallas_call(final_kernel, out_shape=[jax.ShapeDtypeStruct((rows, 4 * D...  40.4 us
    pallas_call x2, Pallas kernels, attention_call(): pl.pallas_call(kernel, grid_spec=pltpu.PrefetchScalarGridSpec(num_scalar_...  39.8 us
    pallas_call x1, Pallas kernels, gather(): pl.pallas_call(gather_kernel, out_shape=[jax.ShapeDtypeStruct((HEADS, row...  30.3 us
    ppermute x1, waiting for transfers between devices, per_device(): lax.ppermute(far, 'seq', [(i + HEADS, i) for i in range(n - HEADS)])  24.6 us
    ppermute x1, waiting for transfers between devices, per_device(): behind = lax.ppermute(jnp.stack([k, v]), 'seq', forward)  23 us
    dot_general x8, matrix products, dot(): lax.dot_general(a, b, dims, precision=precision, preferred_element_type=j...  20.6 us
    reshape x1, local copies, waits for them, and re-layouts, per_device(): w_in.reshape(D, 4, D)  14.6 us
    unnamed x47, local copies, waits for them, and re-layouts  10.3 us
  transfers between devices with their start and end apart: 2, of which 2 were waited for; matrix products, arithmetic and copies ran while one was open for 1% of the time, Pallas kernels for 0%

profile of v1, /device:TPU:15, one launch (start us, length us, event | category | flops | bytes accessed | tf_op | source)
XLA Modules:
  0.0 231.7 jit_solution(12763627306981244209)
XLA Ops:
  0.7 1.4 fusion.1
  2.0 2.0 fusion.2.x_ref
  4.0 14.6 %reshape.49 = bf16[1024,4,1024]{2,1,0:T(4,128)(2,1)} reshape(bf16[1024,4096]{1,0:T(8,128)(2,1)} %param.7) | data formatting | bytes 16777216 | tf_op jit(solution)/shard_map/reshape | solution.py:399
  18.6 1.5 convolution_convert_fusion.dg_ref
  20.2 30.3 %gather.1 = (bf16[8,256,1024]{2,1,0:T(8,128)(2,1)}, bf16[8,256,128]{2,1,0:T(8,128)(2,1)}) custom-call(bf16[256,1024]{1,0:T(8,128)(2,1)} %fusion.2.x_ref, bf16[256,1024]{1,0:T(8,128)(2,1)} %convolution_convert_fusion.dg_ref), custom_call_target="tpu_custom_call" | custom-call | tf_op jit(solution)/shard_map/gather/pallas_call | solution.py:214
  50.4 1.6 constant_dynamic-slice_fusion
  52.0 7.4 %multiply_convert_fusion = (bf16[2048,512]{1,0:T(8,128)(2,1)}, bf16[2048,512]{1,0:T(8,128)(2,1)S(1)}) fusion(bf16[2048,1024]{1,0:T(8,128)(2,1)} %bitcast.61, bf16[128,8,4,128]{3,2,1,0:T(4,128)(2,1)S(1)} %bitcast.68), kind=kOutput, calls=%fused_computation | convolution fusion | flops 2157969408 | bytes 9437184 | tf_op jit(solution)/shard_map/dot_general | solution.py:24
  59.4 1.6 fusion.23
  61.0 1.1 pad_maximum_fusion.1
  62.1 3.5 %collective-permute-start = (bf16[2,2048,128]{2,1,0:T(8,128)(2,1)}, bf16[2,2048,128]{2,1,0:T(8,128)(2,1)S(1)}, u32[]{:S(2)}, u32[]{:S(2)}) collective-permute-start(bf16[2,2048,128]{2,1,0:T(8,128)(2,1)} %pad_maximum_fusion.1), channel_id=1, source_target_pairs={{0,8},{1,9},{2,10},{3,11},{4,12},{5,13},{6,14},{7,15},{8,16},{9,17... | collective-permute-start | bytes 3145736 | tf_op jit(solution)/shard_map/ppermute | solution.py:406
  65.6 0.1 select_reduce_fusion
  65.8 0.2 select_reduce_fusion.1
  66.0 23.0 %collective-permute-done = bf16[2,2048,128]{2,1,0:T(8,128)(2,1)S(1)} collective-permute-done((bf16[2,2048,128]{2,1,0:T(8,128)(2,1)}, bf16[2,2048,128]{2,1,0:T(8,128)(2,1)S(1)}, u32[]{:S(2)}, u32[]{:S(2)}) %collective-permute-start) | collective-permute-done | bytes 1048608 | tf_op jit(solution)/shard_map/ppermute | solution.py:406
  88.9 0.1 slice_bitcast_fusion.2
  89.0 1.5 pad_maximum_fusion.2
  90.5 0.0 copy-done.5
  90.5 0.2 copy-done.10
  90.7 15.0 %attn_fwd.1 = (f32[2048,128]{1,0:T(8,128)S(1)}, f32[2,16,128]{2,1,0:T(8,128)S(1)}) custom-call(s32[16]{0:T(128)S(1)} %get-tuple-element.50.start_ref, s32[16]{0:T(128)S(1)} %get-tuple-element.49.rows_ref, bf16[2048,128]{1,0:T(8,128)(2,1)S(1)} %copy-done.5, bf16[4096,128]{1,0:T(8,128)(2,1)S(1)} %get-tuple-element.51.k_ref, ...), custom_call_target="tpu_custom_call" | custom-call | flops 1000000000 | bytes 4194304 | tf_op jit(solution)/shard_map/attn_fwd/pallas_call | solution.py:373
  105.7 1.0 copy-done.1
  106.7 0.6 copy-done.9
  107.3 1.0 copy-done.12
  108.2 7.3 %stats.1.stat_ref = f32[2,16,128]{2,1,0:T(8,128)} custom-call(f32[2,16,128]{2,1,0:T(8,128)} %copy-done.9), custom_call_target="tpu_custom_call" | custom-call | tf_op jit(solution)/shard_map/stats/pallas_call | solution.py:248
  115.5 1.2 copy-done.2
  116.8 1.0 copy-done.4
  117.8 1.0 copy-done.6
  118.8 0.7 copy-done.8
  119.6 1.0 copy-done.11
  120.6 1.2 copy-done.13
  121.8 24.8 %attn_bwd.1 = (bf16[2048,128]{1,0:T(8,128)(2,1)S(1)}, bf16[2048,128]{1,0:T(8,128)(2,1)S(1)}, f32[2048,128]{1,0:T(8,128)S(1)}, f32[4096,128]{1,0:T(8,128)S(1)}, f32[4096,128]{1,0:T(8,128)S(1)}) custom-call(s32[16]{0:T(128)S(1)} %get-tuple-element.50.start_ref, s32[16]{0:T(128)S(1)} %get-tuple-element.49.rows_ref, bf16[2048,128]{1,0:T(8,128)(2,1)S(1)} %copy-done.6, ...), custom_call_target="tpu_custom_call" | custom-call | flops 2000000000 | bytes 4194304 | tf_op jit(solution)/shard_map/attn_bwd/pallas_call | solution.py:373
  146.7 0.1 fusion.20
  146.7 0.1 fusion.19
  146.8 0.1 pad_maximum_fusion.4
  146.9 0.5 copy-done.7
  147.4 2.2 collective-permute-start.1
  149.7 0.8 convolution_convert_fusion.4
  150.4 0.8 convolution_convert_fusion.2
  151.3 24.6 %collective-permute-done.1 = bf16[2,2048,128]{2,1,0:T(8,128)(2,1)S(1)} collective-permute-done((bf16[2,2048,128]{2,1,0:T(8,128)(2,1)S(1)}, bf16[2,2048,128]{2,1,0:T(8,128)(2,1)S(1)}, u32[]{:S(2)}, u32[]{:S(2)}) %collective-permute-start.1) | collective-permute-done | bytes 1048608 | tf_op jit(solution)/shard_map/ppermute | solution.py:420
  175.9 0.1 convert_element_type.75
  176.0 0.7 fusion.21
  176.7 0.7 convolution_convert_fusion.1
  177.5 0.7 convolution_convert_fusion.3
  178.2 1.1 pad_maximum_fusion.5.w_ref
  179.3 1.6 pad_maximum_fusion.d_ref
  180.9 40.4 %final.1 = (bf16[256,4096]{1,0:T(8,128)(2,1)}, bf16[256,1024]{1,0:T(8,128)(2,1)}, f32[32,1024]{1,0:T(8,128)}) custom-call(bf16[4,2048,128]{2,1,0:T(8,128)(2,1)} %pad_maximum_fusion.d_ref, bf16[2048,128]{1,0:T(8,128)(2,1)} %copy-done.7, bf16[512,1024]{1,0:T(8,128)(2,1)} %pad_maximum_fusion.5.w_ref), custom_call_target="tpu_custom_call" | custom-call | tf_op jit(solution)/shard_map/final/pallas_call | solution.py:340
  221.3 2.7 %fusion = bf16[256,1024]{1,0:T(8,128)(2,1)} fusion(bf16[256,1024]{1,0:T(8,128)(2,1)} %get-tuple-element.24, bf16[1024,1024]{1,0:T(8,128)(2,1)S(1)} %copy-done, bf16[256,1024]{1,0:T(8,128)(2,1)S(1)} %copy-done.16), kind=kOutput, calls=%fused_computation.9 | convolution fusion | flops 537657344 | bytes 3670016 | tf_op jit(solution)/shard_map/dot_general | solution.py:24
  224.0 5.9 %fusion.3 = (f32[256]{0:T(256)S(1)}, f32[256,1024]{1,0:T(8,128)S(1)}) fusion(bf16[256,1024]{1,0:T(8,128)(2,1)S(1)} %copy-done.16, bf16[256,4096]{1,0:T(8,128)(2,1)S(1)} %copy-done.21, bf16[1024,4096]{1,0:T(8,128)(2,1)} %param.7), kind=kOutput, calls=%fused_computation.17 | convolution fusion | flops 2148269824 | bytes 12059648 | tf_op jit(solution)/shard_map/dot_general | solution.py:24
  230.0 1.1 fusion.7
  231.1 0.7 copy.17
  (40 shorter events, 0.1 us)
Async XLA Ops:
  0.6 18.0 %copy-start = (bf16[1024,1024]{1,0:T(8,128)(2,1)S(1)}, bf16[1024,1024]{1,0:T(8,128)(2,1)}, u32[]{:S(2)}) copy-start(bf16[1024,1024]{1,0:T(8,128)(2,1)} %param.8) | copy-start | bytes 6291460
  4.0 14.6 %copy-start.17 = (bf16[256,1024]{1,0:T(8,128)(2,1)S(1)}, bf16[256,1024]{1,0:T(8,128)(2,1)}, u32[]{:S(2)}) copy-start(bf16[256,1024]{1,0:T(8,128)(2,1)} %param.11) | copy-start | bytes 1572868
  61.0 4.6 %copy-start.20 = (s32[64]{0:T(128)S(1)}, s32[64]{0:T(128)}, u32[]{:S(2)}) copy-start(s32[64]{0:T(128)} %param.9) | copy-start | bytes 772
  61.0 4.7 %copy-start.22 = (s32[64]{0:T(128)S(1)}, s32[64]{0:T(128)}, u32[]{:S(2)}) copy-start(s32[64]{0:T(128)} %param.10) | copy-start | bytes 772
  62.1 26.8 %collective-permute-start = (bf16[2,2048,128]{2,1,0:T(8,128)(2,1)}, bf16[2,2048,128]{2,1,0:T(8,128)(2,1)S(1)}, u32[]{:S(2)}, u32[]{:S(2)}) collective-permute-start(bf16[2,2048,128]{2,1,0:T(8,128)(2,1)} %pad_maximum_fusion.1), channel_id=1, source_target_pairs={{0,8},{1,9},{2,10},{3,11},{4,12},{5,13},{6,14},{7,15},{8,16},{9,17... | collective-permute-start | bytes 3145736 | tf_op jit(solution)/shard_map/ppermute | solution.py:406
  89.0 1.5 copy-start.3
  89.0 1.5 copy-start.5
  89.0 1.7 copy-start.10
  105.7 1.0 copy-start.1
  106.6 0.6 copy-start.9
  107.3 1.0 copy-start.12
  115.5 1.2 copy-start.2
  116.8 1.0 copy-start.4
  117.8 1.0 copy-start.6
  118.8 0.7 copy-start.8
  119.6 1.0 copy-start.11
  120.6 1.2 copy-start.13
  121.8 27.8 %copy-start.15 = (bf16[2048,512]{1,0:T(8,128)(2,1)S(1)}, bf16[2048,512]{1,0:T(8,128)(2,1)}, u32[]{:S(2)}) copy-start(bf16[2048,512]{1,0:T(8,128)(2,1)} %get-tuple-element.31) | copy-start | bytes 6291460
  146.6 0.8 copy-start.7
  146.6 3.0 %copy-start.14 = (bf16[8,256,1024]{2,1,0:T(8,128)(2,1)S(1)}, bf16[8,256,1024]{2,1,0:T(8,128)(2,1)}, u32[]{:S(2)}) copy-start(bf16[8,256,1024]{2,1,0:T(8,128)(2,1)} %get-tuple-element.15) | copy-start | bytes 12582916
  147.4 28.5 %collective-permute-start.1 = (bf16[2,2048,128]{2,1,0:T(8,128)(2,1)S(1)}, bf16[2,2048,128]{2,1,0:T(8,128)(2,1)S(1)}, u32[]{:S(2)}, u32[]{:S(2)}) collective-permute-start(bf16[2,2048,128]{2,1,0:T(8,128)(2,1)S(1)} %pad_maximum_fusion.4), channel_id=1, source_target_pairs={{8,0},{9,1},{10,2},{11,3},{12,4},{13,5},{14,6},{15,7},{16,8},{17,9... | collective-permute-start | bytes 3145736 | tf_op jit(solution)/shard_map/ppermute | solution.py:420
  180.9 40.5 %copy-start.16 = (bf16[256,1024]{1,0:T(8,128)(2,1)S(1)}, bf16[256,1024]{1,0:T(8,128)(2,1)}, u32[]{:S(2)}) copy-start(bf16[256,1024]{1,0:T(8,128)(2,1)} %param.6) | copy-start | bytes 1572868
  221.3 2.7 %copy-start.21 = (bf16[256,4096]{1,0:T(8,128)(2,1)S(1)}, bf16[256,4096]{1,0:T(8,128)(2,1)}, u32[]{:S(2)}) copy-start(bf16[256,4096]{1,0:T(8,128)(2,1)} %get-tuple-element.25) | copy-start | bytes 6291460
  224.0 5.9 %copy-start.18 = (bf16[256,1024]{1,0:T(8,128)(2,1)S(1)}, bf16[256,1024]{1,0:T(8,128)(2,1)}, u32[]{:S(2)}) copy-start(bf16[256,1024]{1,0:T(8,128)(2,1)} %param.11) | copy-start | bytes 1572868
  229.9 1.1 copy-start.19

commit v2 on v1

v2 whole, which is shorter than its diff:
```python
import functools

import jax
import jax.numpy as jnp
from jax import lax
from jax.experimental import pallas as pl
from jax.experimental.pallas import tpu as pltpu
from jax.sharding import PartitionSpec as P

MESH = pl.DeviceIdType.MESH
HEADS = 8
HD = 128
BLK = 128
TQ = 256
D = 1024
eps = 1e-05
HALF = 0.5 * HD ** (-0.5)
NT = (((1,), (1,)), ((), ()))
NN = (((1,), (0,)), ((), ()))
TN = (((0,), (0,)), ((), ()))


def dot(a, b, dims, precision=None):
    return lax.dot_general(a, b, dims, precision=precision, preferred_element_type=jnp.float32)


def tile_bounds(start_ref, t, own):
    lo_a, lo_b = start_ref[2 * t], start_ref[2 * t + 1]
    diag = own + t
    return lo_a, lo_b, lo_a // 2, jnp.minimum((lo_b + 1) // 2, diag), diag


def row_valid(rows_ref, t):
    at = lax.broadcasted_iota(jnp.int32, (TQ, HD), 0)
    limit = jnp.where(at < BLK, rows_ref[2 * t], rows_ref[2 * t + 1] + BLK)
    return at < limit


def keep_mask(lo_a, lo_b, diag, kt):
    r = lax.broadcasted_iota(jnp.int32, (TQ, TQ), 0)
    c = lax.broadcasted_iota(jnp.int32, (TQ, TQ), 1) + kt * TQ
    lo = jnp.where(r < BLK, lo_a * BLK, lo_b * BLK)
    return (c >= lo) & (c <= r + diag * TQ)


def fwd_kernel(own, start_ref, rows_ref, q_ref, k_ref, v_ref, u_ref, dg_ref, attn_ref, stat_ref):
    tiles = q_ref.shape[0] // TQ

    @pl.loop(0, tiles)
    def _(t):
        at = pl.ds(pl.multiple_of(t * TQ, TQ), TQ)
        q = jnp.where(row_valid(rows_ref, t), q_ref[at, :], jnp.zeros((), jnp.bfloat16))
        lo_a, lo_b, first, full, diag = tile_bounds(start_ref, t, own)

        def body(masked, kt, acc):
            cols = pl.ds(pl.multiple_of(kt * TQ, TQ), TQ)
            x = dot(q, k_ref[cols, :], NT)
            if masked:
                x = jnp.where(keep_mask(lo_a, lo_b, diag, kt), x, 0.0)
            w = (x + x * jnp.tanh(x)).astype(jnp.bfloat16)
            return acc + dot(w, v_ref[cols, :], NN)

        acc = lax.fori_loop(first, full, functools.partial(body, True), jnp.zeros((TQ, HD), jnp.float32))
        acc = lax.fori_loop(full, diag, functools.partial(body, False), acc)
        acc = body(True, diag, acc) * (1.0 / 2048)
        attn_ref[at, :] = acc
        ones = jnp.ones((8, HD), jnp.float32)
        da = dg_ref[at, :].astype(jnp.float32) * u_ref[at, :].astype(jnp.float32)
        for s, val in enumerate((acc * acc, da * acc)):
            sums = dot(ones, val, NT)
            stat_ref[s, pl.ds(2 * t, 1), :] = sums[0:1, :BLK]
            stat_ref[s, pl.ds(2 * t + 1, 1), :] = sums[0:1, BLK:]


def column(stat, t):
    tall = []
    for half in range(2):
        pick = lax.broadcasted_iota(jnp.int32, (16, HD), 0) == 2 * t + half
        tall.append(dot(stat, pick.astype(jnp.float32), TN, lax.Precision.HIGHEST))
    return jnp.concatenate(tall, axis=0)


def bwd_kernel(own, start_ref, rows_ref, q_ref, k_ref, v_ref, u_ref, dg_ref, attn_ref, stat_ref, slope_ref,
               gated_ref, du_ref, dq_ref, dk_own, dv_own, dk_far, dv_far, dk_ref, dv_ref):
    span = q_ref.shape[0]
    tiles = span // TQ
    dk_ref[...] = jnp.zeros_like(dk_ref)
    dv_ref[...] = jnp.zeros_like(dv_ref)

    @pl.loop(0, tiles)
    def _(t):
        at = pl.ds(pl.multiple_of(t * TQ, TQ), TQ)
        valid = row_valid(rows_ref, t)
        q = jnp.where(valid, q_ref[at, :], jnp.zeros((), jnp.bfloat16))
        square = column(stat_ref[0], t)
        cross = column(stat_ref[1], t)
        r = lax.rsqrt(square * (1.0 / D) + eps)
        attn = attn_ref[at, :]
        u = u_ref[at, :].astype(jnp.float32)
        dg = dg_ref[at, :].astype(jnp.float32)
        na = attn * r
        gated_ref[at, :] = (na * u).astype(gated_ref.dtype)
        du_ref[at, :] = (na * dg * slope_ref[at, :HD].astype(jnp.float32)).astype(du_ref.dtype)
        d_attn = r * (dg * u) - na * (r * r * cross * (1.0 / D))
        do = jnp.where(valid, d_attn, 0.0).astype(jnp.bfloat16)
        lo_a, lo_b, first, full, diag = tile_bounds(start_ref, t, own)

        def body(masked, kt, dq):
            cols = pl.ds(pl.multiple_of(kt * TQ, TQ), TQ)
            k = k_ref[cols, :]
            x = dot(q, k, NT)
            dw = dot(do, v_ref[cols, :], NT)
            a = 1.0 + jnp.tanh(x)
            w = x * a
            ds = dw * (a + w * (2.0 - a))
            if masked:
                keep = keep_mask(lo_a, lo_b, diag, kt)
                w = jnp.where(keep, w, 0.0)
                ds = jnp.where(keep, ds, 0.0)
            w = w.astype(jnp.bfloat16)
            ds = ds.astype(jnp.bfloat16)
            dv_ref[cols, :] += dot(w, do, TN)
            dk_ref[cols, :] += dot(ds, q, TN)
            return dq + dot(ds, k, NN)

        dq = lax.fori_loop(first, full, functools.partial(body, True), jnp.zeros((TQ, HD), jnp.float32))
        dq = lax.fori_loop(full, diag, functools.partial(body, False), dq)
        dq = body(True, diag, dq)
        dq = dq * (HALF / 2048) * slope_ref[at, 2 * HD : 3 * HD].astype(jnp.float32)
        dq_ref[at, :] = dq.astype(dq_ref.dtype)

    for total, far, mine, b in ((dk_ref, dk_far, dk_own, 3), (dv_ref, dv_far, dv_own, 1)):
        far[...] = (total[:span, :] * (1.0 / 2048)).astype(far.dtype)
        mine[...] = total[span:, :] * (1.0 / 2048)


def remote(src, dst, send, recv, device):
    return pltpu.make_async_remote_copy(
        src_ref=src, dst_ref=dst, send_sem=send, recv_sem=recv, device_id=(device,), device_id_type=MESH
    )


def greet(devices):
    barrier = pltpu.get_barrier_semaphore()
    for device in devices:
        pl.semaphore_signal(barrier, inc=1, device_id=(device,), device_id_type=MESH)
    return barrier


def place():
    me = lax.axis_index("seq")
    return me, lax.rem(me, HEADS), me // HEADS


def group_peers(me, pos):
    return [me - pos + lax.rem(pos + step, HEADS) for step in range(1, HEADS)]


def front_kernel(tok_ref, go_ref, win_ref, wout_ref, x_out, q_out, u_out, k_out, v_out, dg_out, slope_out,
                 xs, wh, wo, dgs, w_sem, out_sem, link_s, link_r, core_s, core_r, dg_s, dg_r, kv_s, kv_r):
    me, pos, _ = place()
    n = lax.axis_size("seq")
    base, core, y = me - pos, lax.rem(pos, 2), pos // 2
    rows = tok_ref.shape[0]
    span = rows * HEADS
    peers = group_peers(me, pos)
    after, before = lax.rem(me + HEADS, n), lax.rem(me + n - HEADS, n)
    barrier = greet(peers + [after, before])
    loads = [
        pltpu.make_async_copy(
            win_ref.at[:, pl.ds(pl.multiple_of(b * D + pos * HD, HD), HD)], wh.at[:, pl.ds(b * HD, HD)], w_sem.at[b])
        for b in range(4)
    ]
    loads.append(pltpu.make_async_copy(wout_ref, wo, w_sem.at[4]))
    for copy in loads:
        copy.start()
    xf = tok_ref[...].astype(jnp.float32)
    inv = lax.rsqrt(jnp.mean(xf * xf, axis=-1, keepdims=True) + eps)
    xs[pos] = (xf * inv).astype(jnp.bfloat16)
    half = rows // 2
    halves = [pl.ds(0, half), pl.ds(half, half)]

    def at(step):
        return lax.rem(y + step + 4, 4) * 2 + core

    flip = 1 - 2 * core
    ahead, behind, other = base + at(1), base + at(-1), base + pos + flip
    sent, local = [], []

    def send(src, dst, s, r, device):
        copy = remote(src, dst, s, r, device)
        copy.start()
        sent.append(copy)
        return copy

    pl.semaphore_wait(barrier, len(peers) + 2)
    first = {}
    for h in (0, 1):
        for way, device, part in (("up", ahead, h), ("down", behind, 1 - h)):
            block = xs.at[pos, halves[part]]
            i = 0 if way == "up" else 1
            first[way, part] = send(block, block, link_s.at[i, part], link_r.at[i, part], device)
    cores = [send(xs.at[pos], xs.at[pos], core_s.at[0], core_r.at[0], other)]
    loads[4].wait()
    dgs[...] = dot(go_ref[...], wo[...], NT).astype(jnp.bfloat16)
    mine = pl.ds(pl.multiple_of(pos * rows, rows), rows)
    grads = []
    for i, peer in enumerate(peers):
        to = lax.rem(pos + i + 1, HEADS)
        cols = pl.ds(pl.multiple_of(to * HD, HD), HD)
        grads.append(send(dgs.at[:, cols], dg_out.at[mine], dg_s.at[i], dg_r.at[i], peer))
    dg_out[mine, :] = dgs[:, pl.ds(pl.multiple_of(pos * HD, HD), HD)]
    for copy in loads[:4]:
        copy.wait()
    halo = []

    def process(slot):
        i = len(local)
        local.append(pltpu.make_async_copy(xs.at[slot], x_out.at[slot], out_sem.at[i]))
        local[-1].start()
        pre = dot(xs[slot], wh[...], NN)
        sig = 0.5 + 0.5 * jnp.tanh(0.5 * pre)
        hidden = pre * sig
        where = pl.ds(pl.multiple_of(slot * rows, rows), rows)
        own = pl.ds(pl.multiple_of(span + slot * rows, rows), rows)
        slope_out[where, :] = (sig * (1.0 + pre - hidden)).astype(jnp.bfloat16)
        u_out[where, :] = hidden[:, :HD].astype(jnp.bfloat16)
        v_out[own, :] = hidden[:, HD : 2 * HD].astype(jnp.bfloat16)
        q_out[where, :] = (hidden[:, 2 * HD : 3 * HD] * HALF).astype(jnp.bfloat16)
        k_out[own, :] = hidden[:, 3 * HD :].astype(jnp.bfloat16)
        halo.append(send(k_out.at[own], k_out.at[where], kv_s.at[0, i], kv_r.at[0, i], after))
        halo.append(send(v_out.at[own], v_out.at[where], kv_s.at[1, i], kv_r.at[1, i], after))

    process(pos)
    cores[0].wait_recv()
    process(pos + flip)
    low, high, far = at(-1), at(1), at(2)
    first["up", 0].wait_recv()
    block = xs.at[low, halves[0]]
    second_up = send(block, block, link_s.at[2, 0], link_r.at[2, 0], ahead)
    first["down", 1].wait_recv()
    block = xs.at[high, halves[1]]
    second_down = send(block, block, link_s.at[2, 1], link_r.at[2, 1], behind)
    first["up", 1].wait_recv()
    cores.append(send(xs.at[low], xs.at[low], core_s.at[1], core_r.at[1], other))
    first["down", 0].wait_recv()
    cores.append(send(xs.at[high], xs.at[high], core_s.at[2], core_r.at[2], other))
    process(low)
    process(high)
    cores[1].wait_recv()
    process(low + flip)
    cores[2].wait_recv()
    process(high + flip)
    second_up.wait_recv()
    second_down.wait_recv()
    cores.append(send(xs.at[far], xs.at[far], core_s.at[3], core_r.at[3], other))
    process(far)
    cores[3].wait_recv()
    process(far + flip)
    for copy in grads + halo:
        copy.wait_recv()
    for copy in sent:
        copy.wait_send()
    for copy in local:
        copy.wait()


def front(tokens, grad_out, w_in, w_out):
    rows = tokens.shape[0]
    span = rows * HEADS
    dma = pltpu.SemaphoreType.DMA
    vmem, anywhere = pl.BlockSpec(memory_space=pltpu.VMEM), pl.BlockSpec(memory_space=pl.ANY)

    def shape(*dims):
        return jax.ShapeDtypeStruct(dims, jnp.bfloat16)

    return pl.pallas_call(
        front_kernel,
        out_shape=[shape(HEADS, rows, D), shape(span, HD), shape(span, HD), shape(2 * span, HD),
                   shape(2 * span, HD), shape(span, HD), shape(span, 4 * HD)],
        in_specs=[vmem, vmem, anywhere, anywhere],
        out_specs=[anywhere] + [vmem] * 6,
        scratch_shapes=[
            pltpu.VMEM((HEADS, rows, D), jnp.bfloat16),
            pltpu.VMEM((D, 4 * HD), jnp.bfloat16),
            pltpu.VMEM((D, D), jnp.bfloat16),
            pltpu.VMEM((rows, D), jnp.bfloat16),
            dma((5,)), dma((HEADS,)), dma((3, 2)), dma((3, 2)), dma((4,)), dma((4,)), dma((7,)), dma((7,)),
            dma((2, HEADS)), dma((2, HEADS)),
        ],
        compiler_params=pltpu.CompilerParams(collective_id=1, has_side_effects=True, vmem_limit_bytes=44 * 2**20),
        name="front",
    )(tokens, grad_out, w_in, w_out)


def stats_kernel(s_ref, out_ref, held, send_sem, recv_sem):
    me, pos, _ = place()
    peers = group_peers(me, pos)
    pl.semaphore_wait(greet(peers), len(peers))
    copies = []
    for i, peer in enumerate(peers):
        copy = remote(s_ref, held.at[i], send_sem.at[i], recv_sem.at[i], peer)
        copy.start()
        copies.append(copy)
    total = s_ref[...]
    for i, copy in enumerate(copies):
        copy.wait_recv()
        total = total + held[i]
    out_ref[...] = total
    for copy in copies:
        copy.wait_send()


def sum_stats(stats):
    dma = pltpu.SemaphoreType.DMA
    return pl.pallas_call(
        stats_kernel,
        out_shape=jax.ShapeDtypeStruct(stats.shape, jnp.float32),
        in_specs=[pl.BlockSpec(memory_space=pltpu.VMEM)],
        out_specs=pl.BlockSpec(memory_space=pltpu.VMEM),
        scratch_shapes=[pltpu.VMEM((7,) + stats.shape, jnp.float32), dma((7,)), dma((7,))],
        compiler_params=pltpu.CompilerParams(collective_id=2, has_side_effects=True, vmem_limit_bytes=2 * 2**20),
        name="stats",
    )(stats)


def back_kernel(tok_ref, go_ref, gated_ref, du_ref, dq_ref, dk_ref, dv_ref, kfar_ref, vfar_ref, slope_ref, x_ref, win_ref,
                wout_ref, out_ref, gt_ref, gw_ref, xs, wi, wo, near, d_full, g_full, d_k, d_v, parts, held, total,
                load_sem, move_s, move_r, halo_s, halo_r, late_s, late_r, w_s, w_r, w_own, last_s, last_r, last_own):
    me, pos, group = place()
    n = lax.axis_size("seq")
    groups = held.shape[0]
    rows = tok_ref.shape[0]
    piece = held.shape[1]
    peers = group_peers(me, pos)
    plane = [lax.rem(group + step, groups) * HEADS + pos for step in range(1, groups)]
    after, before = lax.rem(me + HEADS, n), lax.rem(me + n - HEADS, n)
    z, x = group // 4, lax.rem(group, 4)
    dest = lax.rem(x - z + 4, 4) * 32 + pos * 4 + z
    z_from, branch_from = lax.rem(me, 4), me // 32
    source = (z_from * 4 + lax.rem(branch_from + z_from, 4)) * HEADS + lax.rem(me, 32) // 4
    barrier = greet(peers + plane)

    @pl.when(source != me)
    def _():
        pl.semaphore_signal(barrier, inc=1, device_id=(source,), device_id_type=MESH)

    loads = [
        pltpu.make_async_copy(x_ref, xs, load_sem.at[0]),
        pltpu.make_async_copy(wout_ref, wo, load_sem.at[1]),
        pltpu.make_async_copy(win_ref, wi, load_sem.at[2]),
    ]
    for copy in loads:
        copy.start()

    def block(p):
        return pl.ds(pl.multiple_of(p * rows, rows), rows)

    def columns(b):
        return pl.ds(pl.multiple_of(b * D + pos * HD, HD), HD)

    def send(src, dst, s, r, device):
        copy = remote(src, dst, s, r, device)
        copy.start()
        return copy

    pl.semaphore_wait(barrier, len(peers) + len(plane) + jnp.where(dest != me, 1, 0))
    turn = [lax.rem(pos + i + 1, HEADS) for i in range(HEADS)]
    halo = []
    for i, to in enumerate(turn):
        halo.append([
            send(far.at[block(to)], near.at[j, block(to)], halo_s.at[j, i], halo_r.at[j, i], before)
            for j, far in enumerate((kfar_ref, vfar_ref))
        ])
    mine = pl.ds(pl.multiple_of(pos * HD, HD), HD)
    moved = []
    for i, peer in enumerate(peers):
        moved.append([
            send(gated_ref.at[block(turn[i])], g_full.at[:, mine], move_s.at[0, i], move_r.at[0, i], peer),
            send(du_ref.at[block(turn[i])], d_full.at[:, columns(0)], move_s.at[1, i], move_r.at[1, i], peer),
            send(dq_ref.at[block(turn[i])], d_full.at[:, columns(2)], move_s.at[2, i], move_r.at[2, i], peer),
        ])
    g_full[:, mine] = gated_ref[block(pos), :]
    d_full[:, columns(0)] = du_ref[block(pos), :]
    d_full[:, columns(2)] = dq_ref[block(pos), :]

    scattered = []

    def scatter(b, d_ref):
        parts[b] = dot(d_ref[...], xs[...], TN).astype(jnp.bfloat16)
        for sub in range(4):
            to = sub * 4 + (b + sub) % 4
            src = parts.at[b, pl.ds(sub * piece, piece)]
            copy = remote(src, held.at[group], w_s.at[b, sub], w_r.at[group], to * HEADS + pos)

            @pl.when(group != to)
            def _():
                copy.start()

            @pl.when(group == to)
            def _():
                keep = pltpu.make_async_copy(src, held.at[group], w_own)
                keep.start()
                keep.wait()

            scattered.append((to, copy))

    loads[0].wait()
    scatter(0, du_ref)
    scatter(2, dq_ref)
    late = []
    for i, to in enumerate(turn):
        for copy in halo[i]:
            copy.wait_recv()
        here = block(to)
        for j, (own, dst, b) in enumerate(((dk_ref, d_k, 3), (dv_ref, d_v, 1))):
            slope = slope_ref[here, b * HD : (b + 1) * HD].astype(jnp.float32)
            val = ((own[here, :] + near[j, here, :].astype(jnp.float32)) * slope).astype(jnp.bfloat16)
            dst[here, :] = val
            if i < HEADS - 1:
                late.append(send(dst.at[here], d_full.at[:, columns(b)], late_s.at[j, i], late_r.at[j, i], peers[i]))
            else:
                d_full[:, columns(b)] = val
    scatter(3, d_k)
    scatter(1, d_v)
    loads[1].wait()
    for trio in moved:
        trio[0].wait_recv()
    out_ref[...] = (tok_ref[...].astype(jnp.float32) + dot(g_full[...], wo[...], NN)).astype(jnp.bfloat16)
    loads[2].wait()

    def back_dot(b):
        return dot(d_full[:, b * D : (b + 1) * D], wi[:, b * D : (b + 1) * D], NT)

    for trio in moved:
        trio[1].wait_recv()
        trio[2].wait_recv()
    d_normed = back_dot(0) + back_dot(2)
    for copy in late:
        copy.wait_recv()
    d_normed = d_normed + back_dot(3) + back_dot(1)
    xf = tok_ref[...].astype(jnp.float32)
    inv = lax.rsqrt(jnp.mean(xf * xf, axis=-1, keepdims=True) + eps)
    mean = jnp.mean(d_normed * xf, axis=-1, keepdims=True)
    gt_ref[...] = (go_ref[...].astype(jnp.float32) + inv * (d_normed - xf * (inv * inv * mean))).astype(jnp.bfloat16)

    for step in range(1, groups):
        slot = lax.rem(group + step, groups)
        remote(parts.at[0, pl.ds(0, piece)], held.at[slot], w_s.at[0, 0], w_r.at[slot], after).wait_recv()
    acc = held[0].astype(jnp.float32)
    for g in range(1, groups):
        acc = acc + held[g].astype(jnp.float32)
    total[...] = acc

    @pl.when(dest != me)
    def _():
        copy = remote(total, gw_ref, last_s, last_r, dest)
        copy.start()
        copy.wait()

    @pl.when(dest == me)
    def _():
        copy = pltpu.make_async_copy(total, gw_ref, last_own)
        copy.start()
        copy.wait()

    for to, copy in scattered:
        @pl.when(group != to)
        def _():
            copy.wait_send()

    for trio in moved + halo + [late]:
        for copy in trio:
            copy.wait_send()


def back(tokens, grad_out, gated, d_u, d_q, d_k, d_v, k_far, v_far, slope, all_normed, w_in, w_out, groups):
    rows = tokens.shape[0]
    span = rows * HEADS
    dma = pltpu.SemaphoreType.DMA
    piece = 4 * HD // groups
    bf, f32 = jnp.bfloat16, jnp.float32
    vmem, anywhere = pl.BlockSpec(memory_space=pltpu.VMEM), pl.BlockSpec(memory_space=pl.ANY)
    shape = jax.ShapeDtypeStruct
    return pl.pallas_call(
        back_kernel,
        out_shape=[shape((rows, D), bf), shape((rows, D), bf), shape((piece, D), f32)],
        in_specs=[vmem] * 10 + [anywhere] * 3,
        out_specs=[vmem] * 3,
        scratch_shapes=[
            pltpu.VMEM((span, D), bf), pltpu.VMEM((D, 4 * D), bf), pltpu.VMEM((D, D), bf),
            pltpu.VMEM((2, span, HD), bf), pltpu.VMEM((rows, 4 * D), bf), pltpu.VMEM((rows, D), bf),
            pltpu.VMEM((span, HD), bf), pltpu.VMEM((span, HD), bf), pltpu.VMEM((4, HD, D), bf),
            pltpu.VMEM((groups, piece, D), bf), pltpu.VMEM((piece, D), f32),
            dma((3,)), dma((3, 7)), dma((3, 7)), dma((2, HEADS)), dma((2, HEADS)), dma((2, 7)), dma((2, 7)),
            dma((4, 4)), dma((groups,)), dma(()), dma(()), dma(()), dma(()),
        ],
        compiler_params=pltpu.CompilerParams(collective_id=3, has_side_effects=True, vmem_limit_bytes=46 * 2**20),
        name="back",
    )(tokens, grad_out, gated, d_u, d_q, d_k, d_v, k_far, v_far, slope, all_normed, w_in, w_out)


def block_tables(counts, tails, group, own):
    n = counts.shape[0]
    order = jnp.arange(n, dtype=jnp.int32)
    ends = jnp.sum(jnp.where(order[None, :] <= order[:, None], counts[None, :], 0), axis=1)
    blocks = group * own + jnp.arange(own, dtype=jnp.int32)
    starts = ends - counts
    start = jnp.max(jnp.where(starts[None, :] <= blocks[:, None], starts[None, :], 0), axis=1)
    short = jnp.sum(jnp.where(ends[None, :] - 1 == blocks[:, None], tails[None, :] - BLK, 0), axis=1)
    return start - (group - 1) * own, short + BLK


def attention_call(kernel, name, tables, arrays, outs, flops, scratch=()):
    vmem = pl.BlockSpec(memory_space=pltpu.VMEM)
    return pl.pallas_call(
        kernel,
        grid_spec=pltpu.PrefetchScalarGridSpec(
            num_scalar_prefetch=2, grid=(1,), in_specs=[vmem] * len(arrays), out_specs=[vmem] * len(outs),
            scratch_shapes=scratch),
        out_shape=outs,
        compiler_params=pltpu.CompilerParams(vmem_limit_bytes=40 * 2**20),
        cost_estimate=pl.CostEstimate(flops=flops, bytes_accessed=4 * 2**20, transcendentals=2**21),
        name=name,
    )(*tables, *arrays)


def per_device(n, tokens, w_in, w_out, counts, tails, grad_out):
    rows = tokens.shape[0]
    span = rows * HEADS
    groups = n // HEADS
    me, pos, group = place()
    tables = block_tables(counts, tails, group, span // BLK)
    shape = jax.ShapeDtypeStruct
    bf, f32 = jnp.bfloat16, jnp.float32
    all_normed, q, u, k_all, v_all, dg, slope = front(tokens, grad_out, w_in, w_out)
    all_normed = all_normed.reshape(span, D)
    own = span // TQ
    stat_shape = (2, span // BLK, HD)
    attn, stats = attention_call(
        functools.partial(fwd_kernel, own), "attn_fwd", tables, (q, k_all, v_all, u, dg),
        [shape((span, HD), f32), shape(stat_shape, f32)], 10**9)
    stats = sum_stats(stats)
    small, wide = shape((span, HD), bf), shape((span, HD), f32)
    gradients = attention_call(
        functools.partial(bwd_kernel, own), "attn_bwd", tables, (q, k_all, v_all, u, dg, attn, stats, slope),
        [small, small, small, wide, wide, small, small], 2 * 10**9, [pltpu.VMEM((2 * span, HD), f32)] * 2)
    return back(tokens, grad_out, *gradients, slope, all_normed, w_in, w_out, groups)


def solution(mesh):
    in_specs = (P("seq", None), P(), P(), P(), P(), P("seq", None))
    out_specs = (P("seq", None), P("seq", None), P("seq", None))
    return jax.shard_map(
        functools.partial(per_device, mesh.shape["seq"]),
        mesh=mesh, in_specs=in_specs, out_specs=out_specs, check_vma=False,
    )
```

time: 233 us -> 151 us (0.65)
  the two profiles are of different devices: /device:TPU:15 before, /device:TPU:39 now
where the time goes in v2:
time: 151 us; the launch traced here: 149 us
  Pallas kernels  140 us (93%)
  local copies, waits for them, and re-layouts  5.92 us (4%)
  other arithmetic  2.28 us (2%)
    pallas_call x1, Pallas kernels, back(): pl.pallas_call(back_kernel, out_shape=[shape((rows, D), bf), shape((rows,...  81.8 us
    pallas_call x1, Pallas kernels, front(): pl.pallas_call(front_kernel, out_shape=[shape(HEADS, rows, D), shape(span...  35.7 us
    pallas_call x2, Pallas kernels, attention_call(): pl.pallas_call(kernel, grid_spec=pltpu.PrefetchScalarGridSpec(num_scalar_...  16.2 us
    pallas_call x1, Pallas kernels, sum_stats(): pl.pallas_call(stats_kernel, out_shape=jax.ShapeDtypeStruct(stats.shape,...  6.58 us
    unnamed x15, local copies, waits for them, and re-layouts  5.92 us

profile of v2, /device:TPU:39, one launch (start us, length us, event | category | flops | bytes accessed | tf_op | source)
XLA Modules:
  0.0 149.2 jit_solution(11128337395521155573)
XLA Ops:
  0.7 0.7 broadcast_add_fusion.1
  1.3 0.8 select_reduce_fusion
  2.1 0.7 fusion
  2.8 0.2 select_reduce_fusion.1
  2.9 0.0 copy-start
  3.0 1.6 %copy-done = bf16[1024,1024]{1,0:T(8,128)(2,1)S(1)} copy-done((bf16[1024,1024]{1,0:T(8,128)(2,1)S(1)}, bf16[1024,1024]{1,0:T(8,128)(2,1)}, u32[]{:S(2)}) %copy-start) | copy-done | bytes 2097176
  4.5 0.0 copy-start.1
  4.5 1.0 copy-done.1
  5.6 0.0 copy-start.3
  5.6 1.0 copy-done.3
  6.6 35.7 %front.1 = (bf16[8,256,1024]{2,1,0:T(8,128)(2,1)}, bf16[2048,128]{1,0:T(8,128)(2,1)S(1)}, bf16[2048,128]{1,0:T(8,128)(2,1)S(1)}, bf16[4096,128]{1,0:T(8,128)(2,1...) custom-call(bf16[256,1024]{1,0:T(8,128)(2,1)S(1)} %copy-done.1, ...), custom_call_target="tpu_custom_call" | custom-call | tf_op jit(solution)/shard_map/front/pallas_call | solution.py:277
  42.4 0.0 copy-start.5
  42.4 5.6 %attn_fwd.1 = (f32[2048,128]{1,0:T(8,128)S(1)}, f32[2,16,128]{2,1,0:T(8,128)S(1)}) custom-call(s32[16]{0:T(128)S(1)} %get-tuple-element.40.start_ref, s32[16]{0:T(128)S(1)} %get-tuple-element.39.rows_ref, bf16[2048,128]{1,0:T(8,128)(2,1)S(1)} %get-tuple-element.19.q_ref, bf16[4096,128]{1,0:T(8,128)(2,1)S(1)} %get-tuple-element.20.k_ref, ...), custom_call_target="tpu_custom_call" | custom-call | flops 1000000000 | bytes 4194304 | tf_op jit(solution)/shard_map/attn_fwd/pallas_call | solution.py:516
  47.9 0.0 copy-start.2
  47.9 0.0 copy-start.4
  47.9 6.6 %stats.1.stat_ref = f32[2,16,128]{2,1,0:T(8,128)S(1)} custom-call(f32[2,16,128]{2,1,0:T(8,128)S(1)} %get-tuple-element.25.s_ref), custom_call_target="tpu_custom_call" | custom-call | tf_op jit(solution)/shard_map/stats/pallas_call | solution.py:316
  54.5 10.6 %attn_bwd.1 = (bf16[2048,128]{1,0:T(8,128)(2,1)S(1)}, bf16[2048,128]{1,0:T(8,128)(2,1)S(1)}, bf16[2048,128]{1,0:T(8,128)(2,1)S(1)}, f32[2048,128]{1,0:T(8,128)S(...) custom-call(s32[16]{0:T(128)S(1)} %get-tuple-element.40.start_ref, ...), custom_call_target="tpu_custom_call" | custom-call | flops 2000000000 | bytes 4194304 | tf_op jit(solution)/shard_map/attn_bwd/pallas_call | solution.py:516
  65.1 0.0 copy-done.5
  65.2 0.0 copy-done.2
  65.2 0.0 copy-done.4
  65.2 81.8 %back.1 = (bf16[256,1024]{1,0:T(8,128)(2,1)S(1)}, bf16[256,1024]{1,0:T(8,128)(2,1)S(1)}, f32[32,1024]{1,0:T(8,128)S(1)}) custom-call(bf16[256,1024]{1,0:T(8,128)(2,1)S(1)} %copy-done.2, bf16[256,1024]{1,0:T(8,128)(2,1)S(1)} %copy-done.4, bf16[2048,128]{1,0:T(8,128)(2,1)S(1)} %get-tuple-element.27.gated_ref, bf16[2048,128]{1,0:T(8,128)(2,1)S(1)} %get-tuple-element.28.du_ref, ...), custom_call_target="tpu_custom_call" | custom-call | tf_op jit(solution)/shard_map/back/pallas_call | solution.py:485
  146.9 0.8 copy.12
  147.7 0.8 copy.13
  148.5 0.7 copy.14
  (2 shorter events, 0.0 us)
Async XLA Ops:
  2.9 1.6 %copy-start = (bf16[1024,1024]{1,0:T(8,128)(2,1)S(1)}, bf16[1024,1024]{1,0:T(8,128)(2,1)}, u32[]{:S(2)}) copy-start(bf16[1024,1024]{1,0:T(8,128)(2,1)} %wout_ref.3) | copy-start | bytes 6291460
  4.5 1.0 copy-start.1
  5.6 1.0 copy-start.3
  42.4 22.8 %copy-start.5 = (bf16[2048,512]{1,0:T(8,128)(2,1)}, bf16[2048,512]{1,0:T(8,128)(2,1)S(1)}, u32[]{:S(2)}) copy-start(bf16[2048,512]{1,0:T(8,128)(2,1)S(1)} %get-tuple-element.26.slope_ref) | copy-start | bytes 6291460
  47.9 17.2 %copy-start.2 = (bf16[256,1024]{1,0:T(8,128)(2,1)S(1)}, bf16[256,1024]{1,0:T(8,128)(2,1)}, u32[]{:S(2)}) copy-start(bf16[256,1024]{1,0:T(8,128)(2,1)} %tok_ref.3) | copy-start | bytes 1572868
  47.9 17.2 %copy-start.4 = (bf16[256,1024]{1,0:T(8,128)(2,1)S(1)}, bf16[256,1024]{1,0:T(8,128)(2,1)}, u32[]{:S(2)}) copy-start(bf16[256,1024]{1,0:T(8,128)(2,1)} %go_ref.3) | copy-start | bytes 1572868

commit v3 on v2

v3 whole, which is shorter than its diff:
```python
import functools

import jax
import jax.numpy as jnp
from jax import lax
from jax.experimental import pallas as pl
from jax.experimental.pallas import tpu as pltpu
from jax.sharding import PartitionSpec as P

MESH = pl.DeviceIdType.MESH
HEADS = 8
HD = 128
BLK = 128
D = 1024
eps = 1e-05
HALF = 0.5 * HD ** (-0.5)
NT = (((1,), (1,)), ((), ()))
NN = (((1,), (0,)), ((), ()))
TN = (((0,), (0,)), ((), ()))
WIDE = 512
STEP = 256


def dot(a, b, dims):
    return lax.dot_general(a, b, dims, preferred_element_type=jnp.float32)


def group_index():
    return lax.axis_index("seq") // HEADS


def rows_at(start, size):
    return pl.ds(pl.multiple_of(start, BLK), size)


def for_query_tiles(counts_ref, tails_ref, span, visit):
    blocks = span // BLK
    first = group_index() * blocks
    shift = span - first * BLK

    def user(n, begin):
        end = begin + counts_ref[n]
        low, high = jnp.maximum(begin, first), jnp.minimum(end, first + blocks)

        @pl.when(high > low)
        def _():
            count = high - low
            rest = lax.rem(count, 4)
            wide = count // 4 + jnp.where(rest == 3, 1, 0)
            stop = jnp.minimum((end - 1) * BLK + tails_ref[n], high * BLK) + shift
            row, key = low * BLK + shift, begin * BLK + shift
            pl.loop(0, wide)(lambda i: visit(WIDE, row + i * WIDE, key, stop))
            pl.when((rest == 1) | (rest == 2))(lambda: visit(WIDE // 2, row + (count // 4) * WIDE, key, stop))

        return end

    lax.fori_loop(0, counts_ref.shape[0], user, 0)


def valid_rows(size, start, row, stop):
    r = lax.broadcasted_iota(jnp.int32, (size, HD), 0) + start
    return (r >= row) & (r < stop)


def for_key_tiles(size, start, key, body, carry):
    r = lax.broadcasted_iota(jnp.int32, (size, size), 0)
    c = lax.broadcasted_iota(jnp.int32, (size, size), 1)
    back = jnp.maximum(start - key, 0)
    full = back // WIDE

    def plain(j, carry):
        return body(rows_at(start - (j + 1) * WIDE, WIDE), None, carry)

    def part(_, carry):
        end = start - full * WIDE
        base = jnp.maximum(end - WIDE, 0)
        col = lax.broadcasted_iota(jnp.int32, (size, WIDE), 1) + base
        return body(rows_at(base, WIDE), (col >= key) & (col < end), carry)

    carry = lax.fori_loop(0, full, plain, carry)
    carry = lax.fori_loop(0, jnp.where(back > full * WIDE, 1, 0), part, carry)
    return body(rows_at(start, size), (c <= r) & (c >= key - start), carry)


def fwd_kernel(counts_ref, tails_ref, q_ref, kv_ref, u_ref, dg_ref, attn_ref, stat_ref):
    span = q_ref.shape[0]
    attn_ref[...] = jnp.zeros_like(attn_ref)

    def visit(size, row, key, stop):
        start = jnp.minimum(row, 2 * span - size)
        at = rows_at(start - span, size)
        q = jnp.where(valid_rows(size, start, row, stop), q_ref[at, :], jnp.zeros((), jnp.bfloat16))

        def body(cols, keep, acc):
            x = dot(q, kv_ref[cols, :HD], NT)
            if keep is not None:
                x = jnp.where(keep, x, 0.0)
            w = (x + x * jnp.tanh(x)).astype(jnp.bfloat16)
            return acc + dot(w, kv_ref[cols, HD:], NN)

        attn_ref[at, :] += for_key_tiles(size, start, key, body, jnp.zeros((size, HD), jnp.float32)) * (1.0 / 2048)

    for_query_tiles(counts_ref, tails_ref, span, visit)
    ones = jnp.ones((8, HD), jnp.float32)
    for t in range(span // STEP):
        at = pl.ds(t * STEP, STEP)
        acc = attn_ref[at, :]
        da = dg_ref[at, :].astype(jnp.float32) * u_ref[at, :].astype(jnp.float32)
        for s, val in enumerate((acc * acc, da * acc)):
            sums = dot(ones, val, NT)
            for i in range(STEP // BLK):
                stat_ref[s, pl.ds(t * (STEP // BLK) + i, 1), :] = sums[0:1, i * BLK : (i + 1) * BLK]


def bwd_kernel(counts_ref, tails_ref, q_ref, kv_ref, u_ref, dg_ref, attn_ref, stat_ref, slope_ref,
               gated_ref, du_ref, dq_ref, own_ref, far_ref, dk_ref, dv_ref, do_ref, dq_sum):
    span = q_ref.shape[0]
    for ref in (dk_ref, dv_ref, dq_sum):
        ref[...] = jnp.zeros_like(ref)
    r_all = lax.rsqrt(stat_ref[0] * (1.0 / D) + eps)
    c_all = r_all * r_all * r_all * stat_ref[1] * (1.0 / D)
    r_all, c_all = r_all.T, c_all.T
    for t in range(span // BLK):
        at = pl.ds(t * BLK, BLK)
        r, c = (jnp.broadcast_to(val[:, t : t + 1], (BLK, HD)) for val in (r_all, c_all))
        attn = attn_ref[at, :]
        u = u_ref[at, :].astype(jnp.float32)
        dg = dg_ref[at, :].astype(jnp.float32)
        na = attn * r
        gated_ref[at, :] = (na * u).astype(gated_ref.dtype)
        du_ref[at, :] = (na * dg * slope_ref[at, :HD].astype(jnp.float32)).astype(du_ref.dtype)
        do_ref[at, :] = (r * (dg * u) - attn * c).astype(do_ref.dtype)

    def visit(size, row, key, stop):
        start = jnp.minimum(row, 2 * span - size)
        at = rows_at(start - span, size)
        valid = valid_rows(size, start, row, stop)
        q = jnp.where(valid, q_ref[at, :], jnp.zeros((), jnp.bfloat16))
        do = jnp.where(valid, do_ref[at, :], jnp.zeros((), jnp.bfloat16))

        def body(cols, keep, dq):
            k = kv_ref[cols, :HD]
            x = dot(q, k, NT)
            dw = dot(do, kv_ref[cols, HD:], NT)
            a = 1.0 + jnp.tanh(x)
            w = x * a
            ds = dw * (a + w * (2.0 - a))
            if keep is not None:
                w = jnp.where(keep, w, 0.0)
                ds = jnp.where(keep, ds, 0.0)
            w = w.astype(jnp.bfloat16)
            ds = ds.astype(jnp.bfloat16)
            dv_ref[cols, :] += dot(w, do, TN)
            dk_ref[cols, :] += dot(ds, q, TN)
            return dq + dot(ds, k, NN)

        dq_sum[at, :] += for_key_tiles(size, start, key, body, jnp.zeros((size, HD), jnp.float32))

    for_query_tiles(counts_ref, tails_ref, span, visit)
    dq = dq_sum[...] * (HALF / 2048) * slope_ref[:, 2 * HD : 3 * HD].astype(jnp.float32)
    dq_ref[...] = dq.astype(dq_ref.dtype)
    for total, cols in ((dk_ref, slice(0, HD)), (dv_ref, slice(HD, 2 * HD))):
        far_ref[:, cols] = (total[:span, :] * (1.0 / 2048)).astype(far_ref.dtype)
        own_ref[:, cols] = total[span:, :] * (1.0 / 2048)


def remote(src, dst, send, recv, device):
    return pltpu.make_async_remote_copy(
        src_ref=src, dst_ref=dst, send_sem=send, recv_sem=recv, device_id=(device,), device_id_type=MESH
    )


def greet(devices):
    barrier = pltpu.get_barrier_semaphore()
    for device in devices:
        pl.semaphore_signal(barrier, inc=1, device_id=(device,), device_id_type=MESH)
    return barrier


def place():
    me = lax.axis_index("seq")
    return me, lax.rem(me, HEADS), me // HEADS


def group_peers(me, pos):
    return [me - pos + lax.rem(pos + step, HEADS) for step in range(1, HEADS)]


def front_kernel(tok_ref, go_ref, win_ref, wout_ref, x_out, q_out, u_out, kv_out, dg_out, slope_out,
                 tok, go, xs, wh, wo, dgs, slope, load_sem, out_sem, slope_sem, link_s, link_r, core_s, core_r, dg_s, dg_r, kv_s, kv_r):
    me, pos, _ = place()
    n = lax.axis_size("seq")
    base, core, y = me - pos, lax.rem(pos, 2), pos // 2
    rows = tok.shape[0]
    span = rows * HEADS
    half = rows // 2
    peers = group_peers(me, pos)
    after, before = lax.rem(me + HEADS, n), lax.rem(me + n - HEADS, n)
    loads = [pltpu.make_async_copy(tok_ref, tok, load_sem.at[0])]
    loads += [
        pltpu.make_async_copy(
            win_ref.at[:, pl.ds(pl.multiple_of(b * D + pos * HD, HD), HD)], wh.at[:, pl.ds(b * HD, HD)],
            load_sem.at[1 + b])
        for b in range(4)
    ]
    loads += [pltpu.make_async_copy(go_ref, go, load_sem.at[5]), pltpu.make_async_copy(wout_ref, wo, load_sem.at[6])]
    for copy in loads:
        copy.start()
    barrier = greet(peers + [after, before])
    loads[0].wait()
    xf = tok[...].astype(jnp.float32)
    inv = lax.rsqrt(jnp.mean(xf * xf, axis=-1, keepdims=True) + eps)
    xs[pos] = (xf * inv).astype(jnp.bfloat16)

    def at(step):
        return lax.rem(y + step + 4, 4) * 2 + core

    flip = 1 - 2 * core
    ahead, behind, other = base + at(1), base + at(-1), base + pos + flip
    low, high, far = at(-1), at(1), at(2)
    sent, local, halo = [], [], []

    def send(src, dst, s, r, device):
        copy = remote(src, dst, s, r, device)
        copy.start()
        sent.append(copy)
        return copy

    def part(slot, h):
        return xs.at[slot, pl.ds(h * half, half)]

    def link(slot, i, h, device):
        return send(part(slot, h), part(slot, h), link_s.at[i, h], link_r.at[i, h], device)

    def across(slot, i, h):
        return send(part(slot, h), part(slot, h), core_s.at[i, h], core_r.at[i, h], other)

    pl.semaphore_wait(barrier, len(peers) + 2)
    up = {0: link(pos, 0, 0, ahead)}
    down = {1: link(pos, 1, 1, behind)}
    cores = {}
    for h in (0, 1):
        cores[0, h] = across(pos, 0, h)
    up[1] = link(pos, 0, 1, ahead)
    down[0] = link(pos, 1, 0, behind)
    for copy in loads[1:5]:
        copy.wait()

    def process(slot, h, i):
        pre = dot(xs[slot, h * half : (h + 1) * half, :], wh[...], NN)
        sig = 0.5 + 0.5 * jnp.tanh(0.5 * pre)
        hidden = pre * sig
        at_row = pl.multiple_of(slot * rows + h * half, half)
        where, own = pl.ds(at_row, half), pl.ds(pl.multiple_of(span + at_row, half), half)
        kv_out[own, :HD] = hidden[:, 3 * HD :].astype(jnp.bfloat16)
        kv_out[own, HD:] = hidden[:, HD : 2 * HD].astype(jnp.bfloat16)
        copy = remote(kv_out.at[own], kv_out.at[where], kv_s.at[i, h], kv_r.at[i, h], after)
        needed = slot + h > 0
        pl.when(needed)(copy.start)
        halo.append((needed, copy))
        slope[where, :] = (sig * (1.0 + pre - hidden)).astype(jnp.bfloat16)
        local.append(pltpu.make_async_copy(slope.at[where], slope_out.at[where], slope_sem.at[i, h]))
        local[-1].start()
        u_out[where, :] = hidden[:, :HD].astype(jnp.bfloat16)
        q_out[where, :] = (hidden[:, 2 * HD : 3 * HD] * HALF).astype(jnp.bfloat16)

    def keep(slot):
        local.append(pltpu.make_async_copy(xs.at[slot], x_out.at[slot], out_sem.at[slot]))
        local[-1].start()

    for h in (0, 1):
        process(pos, h, 0)
    for h in (0, 1):
        cores[0, h].wait_recv()
        process(pos + flip, h, 1)
    up[0].wait_recv()
    second_up = link(low, 2, 0, ahead)
    cores[1, 0] = across(low, 1, 0)
    down[1].wait_recv()
    second_down = link(high, 2, 1, behind)
    cores[2, 1] = across(high, 2, 1)
    process(low, 0, 2)
    process(high, 1, 3)
    loads[5].wait()
    loads[6].wait()
    dgs[...] = dot(go[...], wo[...], NT).astype(jnp.bfloat16)
    mine = pl.ds(pl.multiple_of(pos * rows, rows), rows)
    grads = []
    for i, peer in enumerate(peers):
        to = lax.rem(pos + i + 1, HEADS)
        cols = pl.ds(pl.multiple_of(to * HD, HD), HD)
        grads.append(send(dgs.at[:, cols], dg_out.at[mine], dg_s.at[i], dg_r.at[i], peer))
    dg_out[mine, :] = dgs[:, pl.ds(pl.multiple_of(pos * HD, HD), HD)]
    cores[1, 0].wait_recv()
    process(low + flip, 0, 4)
    cores[2, 1].wait_recv()
    process(high + flip, 1, 5)
    up[1].wait_recv()
    cores[1, 1] = across(low, 1, 1)
    down[0].wait_recv()
    cores[2, 0] = across(high, 2, 0)
    process(low, 1, 2)
    process(high, 0, 3)
    cores[1, 1].wait_recv()
    process(low + flip, 1, 4)
    cores[2, 0].wait_recv()
    process(high + flip, 0, 5)
    keep(pos)
    keep(pos + flip)
    keep(low)
    keep(high)
    keep(low + flip)
    keep(high + flip)
    second_up.wait_recv()
    cores[3, 0] = across(far, 3, 0)
    second_down.wait_recv()
    cores[3, 1] = across(far, 3, 1)
    for h in (0, 1):
        process(far, h, 6)
    for h in (0, 1):
        cores[3, h].wait_recv()
        process(far + flip, h, 7)
    keep(far)
    keep(far + flip)
    kv_out[:BLK, :] = jnp.zeros((BLK, 2 * HD), jnp.bfloat16)
    for copy in grads:
        copy.wait_recv()
    for needed, copy in halo:
        pl.when(needed)(copy.wait)
    for copy in sent:
        copy.wait_send()
    for copy in local:
        copy.wait()


def front(tokens, grad_out, w_in, w_out):
    rows = tokens.shape[0]
    span = rows * HEADS
    dma = pltpu.SemaphoreType.DMA
    vmem, hbm = pl.BlockSpec(memory_space=pltpu.VMEM), pl.BlockSpec(memory_space=pltpu.HBM)

    def shape(*dims):
        return jax.ShapeDtypeStruct(dims, jnp.bfloat16)

    def scratch(*dims):
        return pltpu.VMEM(dims, jnp.bfloat16)

    return pl.pallas_call(
        front_kernel,
        out_shape=[shape(HEADS, rows, D), shape(span, HD), shape(span, HD), shape(2 * span, 2 * HD),
                   shape(span, HD), shape(span, 4 * HD)],
        in_specs=[hbm] * 4,
        out_specs=[hbm] + [vmem] * 4 + [hbm],
        scratch_shapes=[
            scratch(rows, D), scratch(rows, D), scratch(HEADS, rows, D), scratch(D, 4 * HD), scratch(D, D),
            scratch(rows, D), scratch(span, 4 * HD), dma((7,)), dma((HEADS,)), dma((HEADS, 2)), dma((3, 2)), dma((3, 2)), dma((4, 2)), dma((4, 2)),
            dma((7,)), dma((7,)), dma((HEADS, 2)), dma((HEADS, 2)),
        ],
        compiler_params=pltpu.CompilerParams(collective_id=1, has_side_effects=True, vmem_limit_bytes=48 * 2**20),
        name="front",
    )(tokens, grad_out, w_in, w_out)


def stats_kernel(s_ref, out_ref, held, send_sem, recv_sem):
    me, pos, _ = place()
    peers = group_peers(me, pos)
    pl.semaphore_wait(greet(peers), len(peers))
    copies = []
    for i, peer in enumerate(peers):
        copy = remote(s_ref, held.at[i], send_sem.at[i], recv_sem.at[i], peer)
        copy.start()
        copies.append(copy)
    total = s_ref[...]
    for i, copy in enumerate(copies):
        copy.wait_recv()
        total = total + held[i]
    out_ref[...] = total
    for copy in copies:
        copy.wait_send()


def sum_stats(stats):
    dma = pltpu.SemaphoreType.DMA
    return pl.pallas_call(
        stats_kernel,
        out_shape=jax.ShapeDtypeStruct(stats.shape, jnp.float32),
        in_specs=[pl.BlockSpec(memory_space=pltpu.VMEM)],
        out_specs=pl.BlockSpec(memory_space=pltpu.VMEM),
        scratch_shapes=[pltpu.VMEM((7,) + stats.shape, jnp.float32), dma((7,)), dma((7,))],
        compiler_params=pltpu.CompilerParams(collective_id=2, has_side_effects=True, vmem_limit_bytes=2 * 2**20),
        name="stats",
    )(stats)


def back_kernel(tok_ref, go_ref, gated_ref, du_ref, dq_ref, own_ref, far_ref, slope_ref, x_ref, win_ref,
                wout_ref, out_ref, gt_ref, gw_ref, xs, wi, wo, near, d_full, g_full, d_kv, grads, parts, held, total,
                load_sem, move_s, move_r, halo_s, halo_r, late_s, late_r, w_s, w_r, w_own, last_s, last_r, last_own):
    me, pos, group = place()
    n = lax.axis_size("seq")
    groups = held.shape[0]
    rows = tok_ref.shape[0]
    piece = held.shape[1]
    peers = group_peers(me, pos)
    plane = [lax.rem(group + step, groups) * HEADS + pos for step in range(1, groups)]
    after, before = lax.rem(me + HEADS, n), lax.rem(me + n - HEADS, n)
    z, x = group // 4, lax.rem(group, 4)
    dest = lax.rem(x - z + 4, 4) * 32 + pos * 4 + z
    z_from, branch_from = lax.rem(me, 4), me // 32
    source = (z_from * 4 + lax.rem(branch_from + z_from, 4)) * HEADS + lax.rem(me, 32) // 4
    barrier = greet(peers + plane)

    @pl.when(source != me)
    def _():
        pl.semaphore_signal(barrier, inc=1, device_id=(source,), device_id_type=MESH)

    loads = [
        pltpu.make_async_copy(x_ref, xs, load_sem.at[0]),
        pltpu.make_async_copy(wout_ref, wo, load_sem.at[1]),
        pltpu.make_async_copy(win_ref, wi, load_sem.at[2]),
    ]
    for copy in loads:
        copy.start()

    def block(p):
        return pl.ds(pl.multiple_of(p * rows, rows), rows)

    def columns(b):
        return pl.ds(pl.multiple_of(b * D + pos * HD, HD), HD)

    def send(src, dst, s, r, device):
        copy = remote(src, dst, s, r, device)
        copy.start()
        return copy

    pl.semaphore_wait(barrier, len(peers) + len(plane) + jnp.where(dest != me, 1, 0))
    turn = [lax.rem(pos + i + 1, HEADS) for i in range(HEADS)]
    halo = []
    for i, to in enumerate(turn):
        for h in (0, 1):
            part = pl.ds(pl.multiple_of(to * rows + h * BLK, BLK), BLK)
            copy = remote(far_ref.at[part], near.at[part], halo_s.at[i, h], halo_r.at[i, h], before)
            needed = to + h > 0
            pl.when(needed)(copy.start)
            halo.append((needed, copy))
    near[:BLK, :] = jnp.zeros((BLK, 2 * HD), jnp.bfloat16)
    mine = pl.ds(pl.multiple_of(pos * HD, HD), HD)
    moved = []
    for i, peer in enumerate(peers):
        moved.append([
            send(gated_ref.at[block(turn[i])], g_full.at[:, mine], move_s.at[0, i], move_r.at[0, i], peer),
            send(du_ref.at[block(turn[i])], d_full.at[:, columns(0)], move_s.at[1, i], move_r.at[1, i], peer),
            send(dq_ref.at[block(turn[i])], d_full.at[:, columns(2)], move_s.at[2, i], move_r.at[2, i], peer),
        ])
    g_full[:, mine] = gated_ref[block(pos), :]
    d_full[:, columns(0)] = du_ref[block(pos), :]
    d_full[:, columns(2)] = dq_ref[block(pos), :]

    scattered = []

    def scatter(b, grad):
        parts[b] = grad.astype(jnp.bfloat16)
        for sub in range(4):
            to = sub * 4 + (b + sub) % 4
            src = parts.at[b, pl.ds(sub * piece, piece)]
            copy = remote(src, held.at[group], w_s.at[b, sub], w_r.at[group], to * HEADS + pos)

            @pl.when(group != to)
            def _():
                copy.start()

            @pl.when(group == to)
            def _():
                keep = pltpu.make_async_copy(src, held.at[group], w_own)
                keep.start()
                keep.wait()

            scattered.append((to, copy))

    loads[0].wait()
    scatter(0, dot(du_ref[...], xs[...], TN))
    scatter(2, dot(dq_ref[...], xs[...], TN))
    late = []
    for i, to in enumerate(turn):
        for needed, copy in halo[2 * i : 2 * i + 2]:
            pl.when(needed)(copy.wait_recv)
        here = block(to)
        for j, b in enumerate((3, 1)):
            cols = slice(j * HD, (j + 1) * HD)
            slope = slope_ref[here, b * HD : (b + 1) * HD].astype(jnp.float32)
            val = ((own_ref[here, cols] + near[here, cols].astype(jnp.float32)) * slope).astype(jnp.bfloat16)
            d_kv[j, here, :] = val
            if i < HEADS - 1:
                dst = d_full.at[:, columns(b)]
                late.append(send(d_kv.at[j, here], dst, late_s.at[j, i], late_r.at[j, i], peers[i]))
            else:
                d_full[:, columns(b)] = val
        for j, b in enumerate((3, 1)):
            grad = dot(d_kv[j, here, :], xs[here, :], TN)
            if i == 0:
                grads[j] = grad
            elif i < HEADS - 1:
                grads[j] += grad
            else:
                scatter(b, grads[j] + grad)
    loads[1].wait()
    for trio in moved:
        trio[0].wait_recv()
    out_ref[...] = (tok_ref[...].astype(jnp.float32) + dot(g_full[...], wo[...], NN)).astype(jnp.bfloat16)
    loads[2].wait()

    def back_dot(b):
        return dot(d_full[:, b * D : (b + 1) * D], wi[:, b * D : (b + 1) * D], NT)

    for trio in moved:
        trio[1].wait_recv()
        trio[2].wait_recv()
    d_normed = back_dot(0) + back_dot(2)
    for step in range(1, groups):
        slot = lax.rem(group + step, groups)
        remote(parts.at[0, pl.ds(0, piece)], held.at[slot], w_s.at[0, 0], w_r.at[slot], after).wait_recv()
    acc = held[0].astype(jnp.float32)
    for g in range(1, groups):
        acc = acc + held[g].astype(jnp.float32)
    total[...] = acc
    last = remote(total, gw_ref, last_s, last_r, dest)
    stay = pltpu.make_async_copy(total, gw_ref, last_own)
    pl.when(dest != me)(last.start)
    pl.when(dest == me)(stay.start)
    for copy in late:
        copy.wait_recv()
    d_normed = d_normed + back_dot(3) + back_dot(1)
    xf = tok_ref[...].astype(jnp.float32)
    inv = lax.rsqrt(jnp.mean(xf * xf, axis=-1, keepdims=True) + eps)
    mean = jnp.mean(d_normed * xf, axis=-1, keepdims=True)
    gt_ref[...] = (go_ref[...].astype(jnp.float32) + inv * (d_normed - xf * (inv * inv * mean))).astype(jnp.bfloat16)
    pl.when(dest != me)(last.wait)
    pl.when(dest == me)(stay.wait)
    for to, copy in scattered:
        pl.when(group != to)(copy.wait_send)
    for needed, copy in halo:
        pl.when(needed)(copy.wait_send)
    for copy in [copy for trio in moved for copy in trio] + late:
        copy.wait_send()


def back(tokens, grad_out, gated, d_u, d_q, own, far, slope, all_normed, w_in, w_out, groups):
    rows = tokens.shape[0]
    span = rows * HEADS
    dma = pltpu.SemaphoreType.DMA
    piece = 4 * HD // groups
    bf, f32 = jnp.bfloat16, jnp.float32
    vmem, anywhere = pl.BlockSpec(memory_space=pltpu.VMEM), pl.BlockSpec(memory_space=pl.ANY)
    shape = jax.ShapeDtypeStruct
    return pl.pallas_call(
        back_kernel,
        out_shape=[shape((rows, D), bf), shape((rows, D), bf), shape((piece, D), f32)],
        in_specs=[vmem] * 8 + [anywhere] * 3,
        out_specs=[vmem] * 3,
        scratch_shapes=[
            pltpu.VMEM((span, D), bf), pltpu.VMEM((D, 4 * D), bf), pltpu.VMEM((D, D), bf),
            pltpu.VMEM((span, 2 * HD), bf), pltpu.VMEM((rows, 4 * D), bf), pltpu.VMEM((rows, D), bf),
            pltpu.VMEM((2, span, HD), bf), pltpu.VMEM((2, HD, D), f32), pltpu.VMEM((4, HD, D), bf),
            pltpu.VMEM((groups, piece, D), bf), pltpu.VMEM((piece, D), f32),
            dma((3,)), dma((3, 7)), dma((3, 7)), dma((HEADS, 2)), dma((HEADS, 2)), dma((2, 7)), dma((2, 7)),
            dma((4, 4)), dma((groups,)), dma(()), dma(()), dma(()), dma(()),
        ],
        compiler_params=pltpu.CompilerParams(collective_id=3, has_side_effects=True, vmem_limit_bytes=46 * 2**20),
        name="back",
    )(tokens, grad_out, gated, d_u, d_q, own, far, slope, all_normed, w_in, w_out)


def attention_call(kernel, name, tables, arrays, outs, flops, scratch=()):
    vmem = pl.BlockSpec(memory_space=pltpu.VMEM)
    return pl.pallas_call(
        kernel,
        grid_spec=pltpu.PrefetchScalarGridSpec(
            num_scalar_prefetch=2, grid=(1,), in_specs=[vmem] * len(arrays), out_specs=[vmem] * len(outs),
            scratch_shapes=scratch),
        out_shape=outs,
        compiler_params=pltpu.CompilerParams(vmem_limit_bytes=40 * 2**20),
        cost_estimate=pl.CostEstimate(flops=flops, bytes_accessed=4 * 2**20, transcendentals=2**21),
        name=name,
    )(*tables, *arrays)


def per_device(n, tokens, w_in, w_out, counts, tails, grad_out):
    rows = tokens.shape[0]
    span = rows * HEADS
    shape = jax.ShapeDtypeStruct
    bf, f32 = jnp.bfloat16, jnp.float32
    all_normed, q, u, kv, dg, slope = front(tokens, grad_out, w_in, w_out)
    all_normed = all_normed.reshape(span, D)
    users = (counts, tails)
    attn, stats = attention_call(
        fwd_kernel, "attn_fwd", users, (q, kv, u, dg),
        [shape((span, HD), f32), shape((2, span // BLK, HD), f32)], 10**9)
    stats = sum_stats(stats)
    small, pair = shape((span, HD), bf), (span, 2 * HD)
    both = pltpu.VMEM((2 * span, HD), f32)
    gradients = attention_call(
        bwd_kernel, "attn_bwd", users, (q, kv, u, dg, attn, stats, slope),
        [small, small, small, shape(pair, f32), shape(pair, bf)], 2 * 10**9,
        [both, both, pltpu.VMEM((span, HD), bf), pltpu.VMEM((span, HD), f32)])
    return back(tokens, grad_out, *gradients, slope, all_normed, w_in, w_out, n // HEADS)


def solution(mesh):
    in_specs = (P("seq", None), P(), P(), P(), P(), P("seq", None))
    out_specs = (P("seq", None), P("seq", None), P("seq", None))
    return jax.shard_map(
        functools.partial(per_device, mesh.shape["seq"]),
        mesh=mesh, in_specs=in_specs, out_specs=out_specs, check_vma=False,
    )
```

time: 151 us -> 126 us (0.83)
  the two profiles are of different devices: /device:TPU:39 before, /device:TPU:40 now
where the time goes in v3:
time: 126 us
  Pallas kernels  121 us (96%)
  local copies, waits for them, and re-layouts  4.35 us (3%)
    pallas_call x1, Pallas kernels, back(): pl.pallas_call(back_kernel, out_shape=[shape((rows, D), bf), shape((rows,...  64 us
    pallas_call x1, Pallas kernels, front(): pl.pallas_call(front_kernel, out_shape=[shape(HEADS, rows, D), shape(span...  32.8 us
    pallas_call x2, Pallas kernels, attention_call(): pl.pallas_call(kernel, grid_spec=pltpu.PrefetchScalarGridSpec(num_scalar_...  18 us
    pallas_call x1, Pallas kernels, sum_stats(): pl.pallas_call(stats_kernel, out_shape=jax.ShapeDtypeStruct(stats.shape,...  5.93 us
    unnamed x17, local copies, waits for them, and re-layouts  4.35 us

profile of v3, /device:TPU:40, one launch (start us, length us, event | category | flops | bytes accessed | tf_op | source)
XLA Modules:
  0.0 125.7 jit_solution(10198237448796230025)
XLA Ops:
  0.6 0.0 copy-start
  0.6 1.0 copy-done
  1.7 0.0 copy-start.2
  1.7 1.0 copy-done.2
  2.7 0.0 copy-start.5
  2.7 0.0 copy-start.6
  2.7 32.8 %front.1 = (bf16[8,256,1024]{2,1,0:T(8,128)(2,1)}, bf16[2048,128]{1,0:T(8,128)(2,1)S(1)}, bf16[2048,128]{1,0:T(8,128)(2,1)S(1)}, bf16[4096,256]{1,0:T(8,128)(2,1...) custom-call(bf16[256,1024]{1,0:T(8,128)(2,1)S(1)} %copy-done, bf16[256,1024]{1,0:T(8,128)(2,1)S(1)} %copy-done.2, ...), custom_call_target="tpu_custom_call" | custom-call | tf_op jit(solution)/shard_map/front/pallas_call | solution.py:348
  35.5 0.0 copy-start.4
  35.5 0.0 copy-done.5
  35.5 0.0 copy-done.6
  35.5 6.8 %attn_fwd.1 = (f32[2048,128]{1,0:T(8,128)S(1)}, f32[2,16,128]{2,1,0:T(8,128)S(1)}) custom-call(s32[64]{0:T(128)S(1)} %copy-done.5, s32[64]{0:T(128)S(1)} %copy-done.6, bf16[2048,128]{1,0:T(8,128)(2,1)S(1)} %get-tuple-element.16.q_ref, bf16[4096,256]{1,0:T(8,128)(2,1)S(1)} %get-tuple-element.17.kv_ref, bf16[2048,128]{1,0:T(8,128)(2,1)S(1)} %get-tuple-element.18.u_ref, ...), custom_call_target="tpu_custom_call" | custom-call | flops 1000000000 | bytes 4194304 | tf_op jit(solution)/shard_map/attn_fwd/pallas_call | solution.py:574
  42.3 5.9 %stats.1.stat_ref = f32[2,16,128]{2,1,0:T(8,128)S(1)} custom-call(f32[2,16,128]{2,1,0:T(8,128)S(1)} %get-tuple-element.21.s_ref), custom_call_target="tpu_custom_call" | custom-call | tf_op jit(solution)/shard_map/stats/pallas_call | solution.py:384
  48.2 0.0 copy-done.4
  48.2 0.0 copy-start.1
  48.3 0.0 copy-start.3
  48.3 11.2 %attn_bwd.1 = (bf16[2048,128]{1,0:T(8,128)(2,1)S(1)}, bf16[2048,128]{1,0:T(8,128)(2,1)S(1)}, bf16[2048,128]{1,0:T(8,128)(2,1)S(1)}, f32[2048,256]{1,0:T(8,128)S(1)}, bf16[2048,256]{1,0:T(8,128)(2,1)S(1)}) custom-call(s32[64]{0:T(128)S(1)} %copy-done.5, s32[64]{0:T(128)S(1)} %copy-done.6, bf16[2048,128]{1,0:T(8,128)(2,1)S(1)} %get-tuple-element.16.q_ref, ...), custom_call_target="tpu_custom_call" | custom-call | flops 2000000000 | bytes 4194304 | tf_op jit(solution)/shard_map/attn_bwd/pallas_call | solution.py:574
  59.5 0.0 copy-done.1
  59.5 0.0 copy-done.3
  59.5 64.0 %back.1 = (bf16[256,1024]{1,0:T(8,128)(2,1)S(1)}, bf16[256,1024]{1,0:T(8,128)(2,1)S(1)}, f32[32,1024]{1,0:T(8,128)S(1)}) custom-call(bf16[256,1024]{1,0:T(8,128)(2,1)S(1)} %copy-done.1, bf16[256,1024]{1,0:T(8,128)(2,1)S(1)} %copy-done.3, bf16[2048,128]{1,0:T(8,128)(2,1)S(1)} %get-tuple-element.23.gated_ref, bf16[2048,128]{1,0:T(8,128)(2,1)S(1)} %get-tuple-element.24.du_ref, ...), custom_call_target="tpu_custom_call" | custom-call | tf_op jit(solution)/shard_map/back/pallas_call | solution.py:554
  123.5 0.8 copy.12
  124.3 0.8 copy.13
  125.0 0.7 copy.14
Async XLA Ops:
  0.6 1.0 copy-start
  1.7 1.0 copy-start.2
  2.7 32.8 %copy-start.5 = (s32[64]{0:T(128)S(1)}, s32[64]{0:T(128)}, u32[]{:S(2)}) copy-start(s32[64]{0:T(128)} %counts_ref.3) | copy-start | bytes 772
  2.7 32.8 %copy-start.6 = (s32[64]{0:T(128)S(1)}, s32[64]{0:T(128)}, u32[]{:S(2)}) copy-start(s32[64]{0:T(128)} %tails_ref.3) | copy-start | bytes 772
  35.5 12.7 %copy-start.4 = (bf16[2048,512]{1,0:T(8,128)(2,1)S(1)}, bf16[2048,512]{1,0:T(8,128)(2,1)}, u32[]{:S(2)}) copy-start(bf16[2048,512]{1,0:T(8,128)(2,1)} %get-tuple-element.22.slope_ref) | copy-start | bytes 6291460
  48.2 11.2 %copy-start.1 = (bf16[256,1024]{1,0:T(8,128)(2,1)S(1)}, bf16[256,1024]{1,0:T(8,128)(2,1)}, u32[]{:S(2)}) copy-start(bf16[256,1024]{1,0:T(8,128)(2,1)} %tok_ref.3) | copy-start | bytes 1572868
  48.3 11.2 %copy-start.3 = (bf16[256,1024]{1,0:T(8,128)(2,1)S(1)}, bf16[256,1024]{1,0:T(8,128)(2,1)}, u32[]{:S(2)}) copy-start(bf16[256,1024]{1,0:T(8,128)(2,1)} %go_ref.3) | copy-start | bytes 1572868

commit v4 on v3

--- a/solution.py
+++ b/solution.py
@@ -62,24 +62,32 @@
     return (r >= row) & (r < stop)
 
 
-def for_key_tiles(size, start, key, body, carry):
-    r = lax.broadcasted_iota(jnp.int32, (size, size), 0)
-    c = lax.broadcasted_iota(jnp.int32, (size, size), 1)
+def for_key_tiles(size, start, key, body, diagonal, carry, k_dim):
     back = jnp.maximum(start - key, 0)
     full = back // WIDE
 
+    def index(shape, dim):
+        return lax.broadcasted_iota(jnp.int32, shape, dim)
+
     def plain(j, carry):
-        return body(rows_at(start - (j + 1) * WIDE, WIDE), None, carry)
+        return carry + body(rows_at(start - (j + 1) * WIDE, WIDE), slice(0, size), None)
 
     def part(_, carry):
         end = start - full * WIDE
         base = jnp.maximum(end - WIDE, 0)
-        col = lax.broadcasted_iota(jnp.int32, (size, WIDE), 1) + base
-        return body(rows_at(base, WIDE), (col >= key) & (col < end), carry)
+        col = index((size, WIDE) if k_dim else (WIDE, size), k_dim) + base
+        return carry + body(rows_at(base, WIDE), slice(0, size), (col >= key) & (col < end))
+
+    def piece(q_low, q_high, k_low, k_high):
+        dims = (q_high - q_low, k_high - k_low)
+        dims = dims if k_dim else dims[::-1]
+        r, c = index(dims, 1 - k_dim) + q_low, index(dims, k_dim) + k_low
+        keep = (c <= r) & (c >= key - start)
+        return body(rows_at(start + k_low, k_high - k_low), slice(q_low, q_high), keep)
 
     carry = lax.fori_loop(0, full, plain, carry)
     carry = lax.fori_loop(0, jnp.where(back > full * WIDE, 1, 0), part, carry)
-    return body(rows_at(start, size), (c <= r) & (c >= key - start), carry)
+    return carry + diagonal(piece, size)
 
 
 def fwd_kernel(counts_ref, tails_ref, q_ref, kv_ref, u_ref, dg_ref, attn_ref, stat_ref):
@@ -91,14 +99,18 @@
         at = rows_at(start - span, size)
         q = jnp.where(valid_rows(size, start, row, stop), q_ref[at, :], jnp.zeros((), jnp.bfloat16))
 
-        def body(cols, keep, acc):
-            x = dot(q, kv_ref[cols, :HD], NT)
+        def body(cols, picked, keep):
+            x = dot(q[picked, :], kv_ref[cols, :HD], NT)
             if keep is not None:
                 x = jnp.where(keep, x, 0.0)
             w = (x + x * jnp.tanh(x)).astype(jnp.bfloat16)
-            return acc + dot(w, kv_ref[cols, HD:], NN)
-
-        attn_ref[at, :] += for_key_tiles(size, start, key, body, jnp.zeros((size, HD), jnp.float32)) * (1.0 / 2048)
+            return dot(w, kv_ref[cols, HD:], NN)
+
+        def diagonal(piece, size):
+            return piece(0, size, 0, size)
+
+        acc = for_key_tiles(size, start, key, body, diagonal, jnp.zeros((size, HD), jnp.float32), 1)
+        attn_ref[at, :] += acc * (1.0 / 2048)
 
     for_query_tiles(counts_ref, tails_ref, span, visit)
     ones = jnp.ones((8, HD), jnp.float32)
@@ -138,10 +150,10 @@
         q = jnp.where(valid, q_ref[at, :], jnp.zeros((), jnp.bfloat16))
         do = jnp.where(valid, do_ref[at, :], jnp.zeros((), jnp.bfloat16))
 
-        def body(cols, keep, dq):
-            k = kv_ref[cols, :HD]
-            x = dot(q, k, NT)
-            dw = dot(do, kv_ref[cols, HD:], NT)
+        def body(cols, picked, keep):
+            k, here, d_here = kv_ref[cols, :HD], q[picked, :], do[picked, :]
+            x = dot(k, here, NT)
+            dw = dot(kv_ref[cols, HD:], d_here, NT)
             a = 1.0 + jnp.tanh(x)
             w = x * a
             ds = dw * (a + w * (2.0 - a))
@@ -150,11 +162,19 @@
                 ds = jnp.where(keep, ds, 0.0)
             w = w.astype(jnp.bfloat16)
             ds = ds.astype(jnp.bfloat16)
-            dv_ref[cols, :] += dot(w, do, TN)
-            dk_ref[cols, :] += dot(ds, q, TN)
-            return dq + dot(ds, k, NN)
-
-        dq_sum[at, :] += for_key_tiles(size, start, key, body, jnp.zeros((size, HD), jnp.float32))
+            dv_ref[cols, :] += dot(w, d_here, NN)
+            dk_ref[cols, :] += dot(ds, here, NN)
+            return dot(k, ds, TN)
+
+        def diagonal(piece, size):
+            if size < WIDE:
+                return piece(0, size, 0, size)
+            mid = size // 2
+            early, late = piece(0, size, 0, mid), piece(mid, size, mid, size)
+            return jnp.concatenate([early[:, :mid], early[:, mid:] + late], axis=1)
+
+        dq = for_key_tiles(size, start, key, body, diagonal, jnp.zeros((HD, size), jnp.float32), 0)
+        dq_sum[at, :] += dq.T
 
     for_query_tiles(counts_ref, tails_ref, span, visit)
     dq = dq_sum[...] * (HALF / 2048) * slope_ref[:, 2 * HD : 3 * HD].astype(jnp.float32)
@@ -188,7 +208,7 @@
 
 def front_kernel(tok_ref, go_ref, win_ref, wout_ref, x_out, q_out, u_out, kv_out, dg_out, slope_out,
                  tok, go, xs, wh, wo, dgs, slope, load_sem, out_sem, slope_sem, link_s, link_r, core_s, core_r, dg_s, dg_r, kv_s, kv_r):
-    me, pos, _ = place()
+    me, pos, group = place()
     n = lax.axis_size("seq")
     base, core, y = me - pos, lax.rem(pos, 2), pos // 2
     rows = tok.shape[0]
@@ -206,7 +226,13 @@
     loads += [pltpu.make_async_copy(go_ref, go, load_sem.at[5]), pltpu.make_async_copy(wout_ref, wo, load_sem.at[6])]
     for copy in loads:
         copy.start()
-    barrier = greet(peers + [after, before])
+    barrier = greet(peers)
+    has_before, has_after = group > 0, group < n // HEADS - 1
+    for has, device in ((has_before, before), (has_after, after)):
+        @pl.when(has)
+        def _():
+            pl.semaphore_signal(barrier, inc=1, device_id=(device,), device_id_type=MESH)
+
     loads[0].wait()
     xf = tok[...].astype(jnp.float32)
     inv = lax.rsqrt(jnp.mean(xf * xf, axis=-1, keepdims=True) + eps)
@@ -235,7 +261,7 @@
     def across(slot, i, h):
         return send(part(slot, h), part(slot, h), core_s.at[i, h], core_r.at[i, h], other)
 
-    pl.semaphore_wait(barrier, len(peers) + 2)
+    pl.semaphore_wait(barrier, len(peers) + jnp.where(has_before, 1, 0) + jnp.where(has_after, 1, 0))
     up = {0: link(pos, 0, 0, ahead)}
     down = {1: link(pos, 1, 1, behind)}
     cores = {}
@@ -256,7 +282,7 @@
         kv_out[own, HD:] = hidden[:, HD : 2 * HD].astype(jnp.bfloat16)
         copy = remote(kv_out.at[own], kv_out.at[where], kv_s.at[i, h], kv_r.at[i, h], after)
         needed = slot + h > 0
-        pl.when(needed)(copy.start)
+        pl.when(needed & has_after)(copy.start)
         halo.append((needed, copy))
         slope[where, :] = (sig * (1.0 + pre - hidden)).astype(jnp.bfloat16)
         local.append(pltpu.make_async_copy(slope.at[where], slope_out.at[where], slope_sem.at[i, h]))
@@ -323,10 +349,16 @@
     keep(far)
     keep(far + flip)
     kv_out[:BLK, :] = jnp.zeros((BLK, 2 * HD), jnp.bfloat16)
+
+    @pl.when(group == 0)
+    def _():
+        kv_out[BLK:span, :] = jnp.zeros((span - BLK, 2 * HD), jnp.bfloat16)
+
     for copy in grads:
         copy.wait_recv()
     for needed, copy in halo:
-        pl.when(needed)(copy.wait)
+        pl.when(needed & has_before)(copy.wait_recv)
+        pl.when(needed & has_after)(copy.wait_send)
     for copy in sent:
         copy.wait_send()
     for copy in local:
@@ -393,33 +425,31 @@
 
 
 def back_kernel(tok_ref, go_ref, gated_ref, du_ref, dq_ref, own_ref, far_ref, slope_ref, x_ref, win_ref,
-                wout_ref, out_ref, gt_ref, gw_ref, xs, wi, wo, near, d_full, g_full, d_kv, grads, parts, held, total,
-                load_sem, move_s, move_r, halo_s, halo_r, late_s, late_r, w_s, w_r, w_own, last_s, last_r, last_own):
+                wout_ref, out_ref, gt_ref, gw_ref, xs, wi, wo, near, d_full, g_full, d_kv, grads, parts, held, total, landed,
+                load_sem, move_s, move_r, halo_s, halo_r, late_s, late_r, w_s, w_r, last_s, last_r):
     me, pos, group = place()
     n = lax.axis_size("seq")
-    groups = held.shape[0]
+    groups, piece = held.shape[1] + 1, held.shape[2]
     rows = tok_ref.shape[0]
-    piece = held.shape[1]
     peers = group_peers(me, pos)
     plane = [lax.rem(group + step, groups) * HEADS + pos for step in range(1, groups)]
     after, before = lax.rem(me + HEADS, n), lax.rem(me + n - HEADS, n)
-    z, x = group // 4, lax.rem(group, 4)
-    dest = lax.rem(x - z + 4, 4) * 32 + pos * 4 + z
-    z_from, branch_from = lax.rem(me, 4), me // 32
-    source = (z_from * 4 + lax.rem(branch_from + z_from, 4)) * HEADS + lax.rem(me, 32) // 4
+    has_before, has_after = group > 0, group < groups - 1
+    dests = [(2 * (group // 8) + r) * 32 + pos * 4 + lax.rem(group, 8) // 2 for r in range(2)]
+    sources = [((me // 64) * 8 + 2 * lax.rem(me, 4) + i) * HEADS + lax.rem(me, 32) // 4 for i in range(2)]
     barrier = greet(peers + plane)
-
-    @pl.when(source != me)
-    def _():
-        pl.semaphore_signal(barrier, inc=1, device_id=(source,), device_id_type=MESH)
+    for source in sources:
+        @pl.when(source != me)
+        def _():
+            pl.semaphore_signal(barrier, inc=1, device_id=(source,), device_id_type=MESH)
 
     loads = [
         pltpu.make_async_copy(x_ref, xs, load_sem.at[0]),
         pltpu.make_async_copy(wout_ref, wo, load_sem.at[1]),
         pltpu.make_async_copy(win_ref, wi, load_sem.at[2]),
     ]
-    for copy in loads:
-        copy.start()
+    loads[0].start()
+    loads[1].start()
 
     def block(p):
         return pl.ds(pl.multiple_of(p * rows, rows), rows)
@@ -432,7 +462,7 @@
         copy.start()
         return copy
 
-    pl.semaphore_wait(barrier, len(peers) + len(plane) + jnp.where(dest != me, 1, 0))
+    pl.semaphore_wait(barrier, len(peers) + len(plane) + sum(jnp.where(dest != me, 1, 0) for dest in dests))
     turn = [lax.rem(pos + i + 1, HEADS) for i in range(HEADS)]
     halo = []
     for i, to in enumerate(turn):
@@ -440,9 +470,14 @@
             part = pl.ds(pl.multiple_of(to * rows + h * BLK, BLK), BLK)
             copy = remote(far_ref.at[part], near.at[part], halo_s.at[i, h], halo_r.at[i, h], before)
             needed = to + h > 0
-            pl.when(needed)(copy.start)
+            pl.when(needed & has_before)(copy.start)
             halo.append((needed, copy))
     near[:BLK, :] = jnp.zeros((BLK, 2 * HD), jnp.bfloat16)
+
+    @pl.when(jnp.logical_not(has_after))
+    def _():
+        near[BLK:, :] = jnp.zeros((near.shape[0] - BLK, 2 * HD), jnp.bfloat16)
+
     mine = pl.ds(pl.multiple_of(pos * HD, HD), HD)
     moved = []
     for i, peer in enumerate(peers):
@@ -457,51 +492,64 @@
 
     scattered = []
 
-    def scatter(b, grad):
-        parts[b] = grad.astype(jnp.bfloat16)
-        for sub in range(4):
-            to = sub * 4 + (b + sub) % 4
-            src = parts.at[b, pl.ds(sub * piece, piece)]
-            copy = remote(src, held.at[group], w_s.at[b, sub], w_r.at[group], to * HEADS + pos)
-
-            @pl.when(group != to)
-            def _():
-                copy.start()
-
-            @pl.when(group == to)
-            def _():
-                keep = pltpu.make_async_copy(src, held.at[group], w_own)
-                keep.start()
-                keep.wait()
-
-            scattered.append((to, copy))
+    def fill(r, pair):
+        for j, grad in enumerate(pair):
+            parts[r, j * HD : (j + 1) * HD, :] = grad.astype(jnp.bfloat16)
+
+    def share(index, size):
+        return pl.ds(pl.multiple_of(index * size, piece), size)
+
+    def scatter(r):
+        for i, peer in enumerate(plane):
+            to = lax.rem(group + i + 1, groups)
+            scattered.append(send(parts.at[r, share(to, piece)], held.at[r, i], w_s.at[r, i], w_r.at[r, i], peer))
+
+    def collect(r):
+        acc = parts[r, share(group, piece), :].astype(jnp.float32)
+        for i in range(groups - 1):
+            scattered[r * (groups - 1) + i].wait_recv()
+            acc = acc + held[r, i].astype(jnp.float32)
+        return acc
+
+    half = share(lax.rem(group, 2), piece)
+
+    def pass_on(r, acc):
+        total[r] = acc.astype(jnp.bfloat16)
+        copy = remote(total.at[r], landed.at[half], last_s.at[r], last_r.at[lax.rem(group, 2)], dests[r])
+        pl.when(dests[r] != me)(copy.start)
+
+        @pl.when(dests[r] == me)
+        def _():
+            landed[half, :] = total[r]
+
+        return copy
 
     loads[0].wait()
-    scatter(0, dot(du_ref[...], xs[...], TN))
-    scatter(2, dot(dq_ref[...], xs[...], TN))
+    loads[2].start()
+    grad = dot(jnp.concatenate([du_ref[...], dq_ref[...]], axis=1), xs[...], TN)
+    fill(0, [grad[:HD], grad[HD:]])
+    scatter(0)
     late = []
     for i, to in enumerate(turn):
         for needed, copy in halo[2 * i : 2 * i + 2]:
-            pl.when(needed)(copy.wait_recv)
+            pl.when(needed & has_after)(copy.wait_recv)
         here = block(to)
-        for j, b in enumerate((3, 1)):
+        for j, b in ((0, 3), (1, 1)):
             cols = slice(j * HD, (j + 1) * HD)
             slope = slope_ref[here, b * HD : (b + 1) * HD].astype(jnp.float32)
             val = ((own_ref[here, cols] + near[here, cols].astype(jnp.float32)) * slope).astype(jnp.bfloat16)
-            d_kv[j, here, :] = val
+            d_kv[here, cols] = val
             if i < HEADS - 1:
                 dst = d_full.at[:, columns(b)]
-                late.append(send(d_kv.at[j, here], dst, late_s.at[j, i], late_r.at[j, i], peers[i]))
+                late.append(send(d_kv.at[here, cols], dst, late_s.at[j, i], late_r.at[j, i], peers[i]))
             else:
                 d_full[:, columns(b)] = val
-        for j, b in enumerate((3, 1)):
-            grad = dot(d_kv[j, here, :], xs[here, :], TN)
-            if i == 0:
-                grads[j] = grad
-            elif i < HEADS - 1:
-                grads[j] += grad
-            else:
-                scatter(b, grads[j] + grad)
+        grad = dot(d_kv[here, :], xs[here, :], TN)
+        if i < HEADS - 1:
+            grads[...] = grad if i == 0 else grads[...] + grad
+    grad = grads[...] + grad
+    fill(1, [grad[HD:], grad[:HD]])
+    scatter(1)
     loads[1].wait()
     for trio in moved:
         trio[0].wait_recv()
@@ -515,17 +563,7 @@
         trio[1].wait_recv()
         trio[2].wait_recv()
     d_normed = back_dot(0) + back_dot(2)
-    for step in range(1, groups):
-        slot = lax.rem(group + step, groups)
-        remote(parts.at[0, pl.ds(0, piece)], held.at[slot], w_s.at[0, 0], w_r.at[slot], after).wait_recv()
-    acc = held[0].astype(jnp.float32)
-    for g in range(1, groups):
-        acc = acc + held[g].astype(jnp.float32)
-    total[...] = acc
-    last = remote(total, gw_ref, last_s, last_r, dest)
-    stay = pltpu.make_async_copy(total, gw_ref, last_own)
-    pl.when(dest != me)(last.start)
-    pl.when(dest == me)(stay.start)
+    last = [pass_on(0, collect(0)), pass_on(1, collect(1))]
     for copy in late:
         copy.wait_recv()
     d_normed = d_normed + back_dot(3) + back_dot(1)
@@ -533,13 +571,16 @@
     inv = lax.rsqrt(jnp.mean(xf * xf, axis=-1, keepdims=True) + eps)
     mean = jnp.mean(d_normed * xf, axis=-1, keepdims=True)
     gt_ref[...] = (go_ref[...].astype(jnp.float32) + inv * (d_normed - xf * (inv * inv * mean))).astype(jnp.bfloat16)
-    pl.when(dest != me)(last.wait)
-    pl.when(dest == me)(stay.wait)
-    for to, copy in scattered:
-        pl.when(group != to)(copy.wait_send)
+    for i, source in enumerate(sources):
+        rows_i = landed.at[pl.ds(i * piece, piece)]
+        copy = remote(total.at[0], rows_i, last_s.at[0], last_r.at[i], after)
+        pl.when(source != me)(copy.wait_recv)
+    gw_ref[...] = landed[...].astype(jnp.float32)
+    for dest, copy in zip(dests, last):
+        pl.when(dest != me)(copy.wait_send)
     for needed, copy in halo:
-        pl.when(needed)(copy.wait_send)
-    for copy in [copy for trio in moved for copy in trio] + late:
+        pl.when(needed & has_before)(copy.wait_send)
+    for copy in [copy for trio in moved for copy in trio] + late + scattered:
         copy.wait_send()
 
 
@@ -547,22 +588,22 @@
     rows = tokens.shape[0]
     span = rows * HEADS
     dma = pltpu.SemaphoreType.DMA
-    piece = 4 * HD // groups
+    piece = 2 * HD // groups
     bf, f32 = jnp.bfloat16, jnp.float32
     vmem, anywhere = pl.BlockSpec(memory_space=pltpu.VMEM), pl.BlockSpec(memory_space=pl.ANY)
     shape = jax.ShapeDtypeStruct
     return pl.pallas_call(
         back_kernel,
-        out_shape=[shape((rows, D), bf), shape((rows, D), bf), shape((piece, D), f32)],
+        out_shape=[shape((rows, D), bf), shape((rows, D), bf), shape((2 * piece, D), f32)],
         in_specs=[vmem] * 8 + [anywhere] * 3,
         out_specs=[vmem] * 3,
         scratch_shapes=[
             pltpu.VMEM((span, D), bf), pltpu.VMEM((D, 4 * D), bf), pltpu.VMEM((D, D), bf),
             pltpu.VMEM((span, 2 * HD), bf), pltpu.VMEM((rows, 4 * D), bf), pltpu.VMEM((rows, D), bf),
-            pltpu.VMEM((2, span, HD), bf), pltpu.VMEM((2, HD, D), f32), pltpu.VMEM((4, HD, D), bf),
-            pltpu.VMEM((groups, piece, D), bf), pltpu.VMEM((piece, D), f32),
+            pltpu.VMEM((span, 2 * HD), bf), pltpu.VMEM((2 * HD, D), f32), pltpu.VMEM((2, 2 * HD, D), bf),
+            pltpu.VMEM((2, groups - 1, piece, D), bf), pltpu.VMEM((2, piece, D), bf), pltpu.VMEM((2 * piece, D), bf),
             dma((3,)), dma((3, 7)), dma((3, 7)), dma((HEADS, 2)), dma((HEADS, 2)), dma((2, 7)), dma((2, 7)),
-            dma((4, 4)), dma((groups,)), dma(()), dma(()), dma(()), dma(()),
+            dma((2, groups - 1)), dma((2, groups - 1)), dma((2,)), dma((2,)),
         ],
         compiler_params=pltpu.CompilerParams(collective_id=3, has_side_effects=True, vmem_limit_bytes=46 * 2**20),
         name="back",
@@ -588,7 +629,7 @@
     span = rows * HEADS
     shape = jax.ShapeDtypeStruct
     bf, f32 = jnp.bfloat16, jnp.float32
-    all_normed, q, u, kv, dg, slope = front(tokens, grad_out, w_in, w_out)
+    all_normed, q, u, kv, dg, slope = front(*(pltpu.with_memory_space_constraint(a, pltpu.HBM) for a in (tokens, grad_out, w_in, w_out)))
     all_normed = all_normed.reshape(span, D)
     users = (counts, tails)
     attn, stats = attention_call(

time: 126 us -> 116 us (0.921)
  the two profiles are of different devices: /device:TPU:40 before, /device:TPU:39 now
where the time goes in v4:
time: 116 us
  Pallas kernels  113 us (97%)
  local copies, waits for them, and re-layouts  2.27 us (2%)
    pallas_call x1, Pallas kernels, back(): pl.pallas_call(back_kernel, out_shape=[shape((rows, D), bf), shape((rows,...  51.9 us
    pallas_call x1, Pallas kernels, front(): pl.pallas_call(front_kernel, out_shape=[shape(HEADS, rows, D), shape(span...  30.4 us
    pallas_call x2, Pallas kernels, attention_call(): pl.pallas_call(kernel, grid_spec=pltpu.PrefetchScalarGridSpec(num_scalar_...  22 us
    pallas_call x1, Pallas kernels, sum_stats(): pl.pallas_call(stats_kernel, out_shape=jax.ShapeDtypeStruct(stats.shape,...  8.61 us

profile of v4, /device:TPU:39, one launch (start us, length us, event | category | flops | bytes accessed | tf_op | source)
XLA Modules:
  0.0 115.9 jit_solution(18090784399709144347)
XLA Ops:
  0.6 0.0 copy-start.4
  0.6 0.0 copy-start.3
  0.7 30.4 %front.1 = (bf16[8,256,1024]{2,1,0:T(8,128)(2,1)}, bf16[2048,128]{1,0:T(8,128)(2,1)S(1)}, bf16[2048,128]{1,0:T(8,128)(2,1)S(1)}, bf16[4096,256]{1,0:T(8,128)(2,1...) custom-call(bf16[256,1024]{1,0:T(8,128)(2,1)} %tok_ref.3, bf16[256,1024]{1,0:T(8,128)(2,1)} %go_ref.3, ...), custom_call_target="tpu_custom_call" | custom-call | tf_op jit(solution)/shard_map/front/pallas_call | solution.py:380
  31.0 0.0 copy-start.2
  31.0 0.0 copy-done.4
  31.1 0.0 copy-done.3
  31.1 8.2 %attn_fwd.1 = (f32[2048,128]{1,0:T(8,128)S(1)}, f32[2,16,128]{2,1,0:T(8,128)S(1)}) custom-call(s32[64]{0:T(128)S(1)} %copy-done.3, s32[64]{0:T(128)S(1)} %copy-done.4, bf16[2048,128]{1,0:T(8,128)(2,1)S(1)} %get-tuple-element.16.q_ref, bf16[4096,256]{1,0:T(8,128)(2,1)S(1)} %get-tuple-element.17.kv_ref, bf16[2048,128]{1,0:T(8,128)(2,1)S(1)} %get-tuple-element.18.u_ref, ...), custom_call_target="tpu_custom_call" | custom-call | flops 1000000000 | bytes 4194304 | tf_op jit(solution)/shard_map/attn_fwd/pallas_call | solution.py:615
  39.2 8.6 %stats.1.stat_ref = f32[2,16,128]{2,1,0:T(8,128)S(1)} custom-call(f32[2,16,128]{2,1,0:T(8,128)S(1)} %get-tuple-element.21.s_ref), custom_call_target="tpu_custom_call" | custom-call | tf_op jit(solution)/shard_map/stats/pallas_call | solution.py:416
  47.9 0.0 copy-start
  47.9 0.0 copy-start.1
  47.9 13.8 %attn_bwd.1 = (bf16[2048,128]{1,0:T(8,128)(2,1)S(1)}, bf16[2048,128]{1,0:T(8,128)(2,1)S(1)}, bf16[2048,128]{1,0:T(8,128)(2,1)S(1)}, f32[2048,256]{1,0:T(8,128)S(1)}, bf16[2048,256]{1,0:T(8,128)(2,1)S(1)}) custom-call(s32[64]{0:T(128)S(1)} %copy-done.3, s32[64]{0:T(128)S(1)} %copy-done.4, bf16[2048,128]{1,0:T(8,128)(2,1)S(1)} %get-tuple-element.16.q_ref, ...), custom_call_target="tpu_custom_call" | custom-call | flops 2000000000 | bytes 4194304 | tf_op jit(solution)/shard_map/attn_bwd/pallas_call | solution.py:615
  61.7 0.0 copy-done.2
  61.8 0.0 copy-done
  61.8 0.0 copy-done.1
  61.8 51.9 %back.1 = (bf16[256,1024]{1,0:T(8,128)(2,1)S(1)}, bf16[256,1024]{1,0:T(8,128)(2,1)S(1)}, f32[32,1024]{1,0:T(8,128)S(1)}) custom-call(bf16[256,1024]{1,0:T(8,128)(2,1)S(1)} %copy-done, bf16[256,1024]{1,0:T(8,128)(2,1)S(1)} %copy-done.1, bf16[2048,128]{1,0:T(8,128)(2,1)S(1)} %get-tuple-element.23.gated_ref, bf16[2048,128]{1,0:T(8,128)(2,1)S(1)} %get-tuple-element.24.du_ref, ...), custom_call_target="tpu_custom_call" | custom-call | tf_op jit(solution)/shard_map/back/pallas_call | solution.py:595
  113.6 0.8 copy.12
  114.4 0.8 copy.13
  115.2 0.7 copy.14
Async XLA Ops:
  0.6 30.4 %copy-start.4 = (s32[64]{0:T(128)S(1)}, s32[64]{0:T(128)}, u32[]{:S(2)}) copy-start(s32[64]{0:T(128)} %tails_ref.3) | copy-start | bytes 772
  0.6 30.4 %copy-start.3 = (s32[64]{0:T(128)S(1)}, s32[64]{0:T(128)}, u32[]{:S(2)}) copy-start(s32[64]{0:T(128)} %counts_ref.3) | copy-start | bytes 772
  31.0 30.7 %copy-start.2 = (bf16[2048,512]{1,0:T(8,128)(2,1)}, bf16[2048,512]{1,0:T(8,128)(2,1)S(1)}, u32[]{:S(2)}) copy-start(bf16[2048,512]{1,0:T(8,128)(2,1)S(1)} %get-tuple-element.22.slope_ref) | copy-start | bytes 6291460
  47.9 13.9 %copy-start = (bf16[256,1024]{1,0:T(8,128)(2,1)S(1)}, bf16[256,1024]{1,0:T(8,128)(2,1)}, u32[]{:S(2)}) copy-start(bf16[256,1024]{1,0:T(8,128)(2,1)} %tok_ref.3) | copy-start | bytes 1572868
  47.9 13.9 %copy-start.1 = (bf16[256,1024]{1,0:T(8,128)(2,1)S(1)}, bf16[256,1024]{1,0:T(8,128)(2,1)}, u32[]{:S(2)}) copy-start(bf16[256,1024]{1,0:T(8,128)(2,1)} %go_ref.3) | copy-start | bytes 1572868

commit v5 on v4

--- a/solution.py
+++ b/solution.py
@@ -44,13 +44,15 @@
 
         @pl.when(high > low)
         def _():
-            count = high - low
-            rest = lax.rem(count, 4)
-            wide = count // 4 + jnp.where(rest == 3, 1, 0)
-            stop = jnp.minimum((end - 1) * BLK + tails_ref[n], high * BLK) + shift
-            row, key = low * BLK + shift, begin * BLK + shift
-            pl.loop(0, wide)(lambda i: visit(WIDE, row + i * WIDE, key, stop))
-            pl.when((rest == 1) | (rest == 2))(lambda: visit(WIDE // 2, row + (count // 4) * WIDE, key, stop))
+            top = jnp.minimum((end - 1) * BLK + tails_ref[n], high * BLK) + shift
+
+            @pl.loop((low - begin) // 4, (high - begin + 3) // 4)
+            def _(tile):
+                near = jnp.maximum(begin + 4 * tile, low)
+                past = jnp.minimum(begin + 4 * tile + 4, high)
+                row, stop = near * BLK + shift, jnp.minimum(top, past * BLK + shift)
+                pl.when(past - near > 2)(lambda: visit(WIDE, row, begin * BLK + shift, stop))
+                pl.when(past - near <= 2)(lambda: visit(WIDE // 2, row, begin * BLK + shift, stop))
 
         return end
 
@@ -85,7 +87,13 @@
         keep = (c <= r) & (c >= key - start)
         return body(rows_at(start + k_low, k_high - k_low), slice(q_low, q_high), keep)
 
-    carry = lax.fori_loop(0, full, plain, carry)
+    pairs = full // 2 if k_dim == 0 else 0
+
+    def pair(j, carry):
+        return carry + body(rows_at(start - (j + 1) * 2 * WIDE, 2 * WIDE), slice(0, size), None)
+
+    carry = lax.fori_loop(0, pairs, pair, carry)
+    carry = lax.fori_loop(2 * pairs, full, plain, carry)
     carry = lax.fori_loop(0, jnp.where(back > full * WIDE, 1, 0), part, carry)
     return carry + diagonal(piece, size)
 
@@ -610,6 +618,28 @@
     )(tokens, grad_out, gated, d_u, d_q, own, far, slope, all_normed, w_in, w_out)
 
 
+def store_kernel(*refs):
+    count = len(refs) // 2
+    sems = refs[-1]
+    copies = [pltpu.make_async_copy(refs[i], refs[count + i], sems.at[i]) for i in range(count)]
+    for copy in copies:
+        copy.start()
+    for copy in copies:
+        copy.wait()
+
+
+def store(*arrays):
+    return pl.pallas_call(
+        store_kernel,
+        out_shape=[jax.ShapeDtypeStruct(a.shape, a.dtype) for a in arrays],
+        in_specs=[pl.BlockSpec(memory_space=pltpu.VMEM)] * len(arrays),
+        out_specs=[pl.BlockSpec(memory_space=pltpu.HBM)] * len(arrays),
+        scratch_shapes=[pltpu.SemaphoreType.DMA((len(arrays),))],
+        compiler_params=pltpu.CompilerParams(vmem_limit_bytes=2 * 2**20),
+        name="store",
+    )(*arrays)
+
+
 def attention_call(kernel, name, tables, arrays, outs, flops, scratch=()):
     vmem = pl.BlockSpec(memory_space=pltpu.VMEM)
     return pl.pallas_call(
@@ -642,7 +672,7 @@
         bwd_kernel, "attn_bwd", users, (q, kv, u, dg, attn, stats, slope),
         [small, small, small, shape(pair, f32), shape(pair, bf)], 2 * 10**9,
         [both, both, pltpu.VMEM((span, HD), bf), pltpu.VMEM((span, HD), f32)])
-    return back(tokens, grad_out, *gradients, slope, all_normed, w_in, w_out, n // HEADS)
+    return store(*back(tokens, grad_out, *gradients, slope, all_normed, w_in, w_out, n // HEADS))
 
 
 def solution(mesh):

time: 116 us -> 110 us (0.948)
  Pallas kernels: 113 us -> 109 us
  local copies, waits for them, and re-layouts: 2.27 us -> 0.03 us
    pallas_call x2, Pallas kernels: 22 us -> 16.1 us  [attention_call(): pl.pallas_call(kernel, grid_spec=pltpu.PrefetchScalarGridSpec(num_scalar_...]
    unnamed x13 -> x10, local copies, waits for them, and re-layouts: 2.27 us -> 0.03 us
where the time goes in v5:
time: 110 us
  Pallas kernels  109 us (99%)
    pallas_call x1, Pallas kernels, back(): pl.pallas_call(back_kernel, out_shape=[shape((rows, D), bf), shape((rows,...  52.6 us
    pallas_call x1, Pallas kernels, front(): pl.pallas_call(front_kernel, out_shape=[shape(HEADS, rows, D), shape(span...  30.4 us
    pallas_call x2, Pallas kernels, attention_call(): pl.pallas_call(kernel, grid_spec=pltpu.PrefetchScalarGridSpec(num_scalar_...  16.1 us
    pallas_call x1, Pallas kernels, sum_stats(): pl.pallas_call(stats_kernel, out_shape=jax.ShapeDtypeStruct(stats.shape,...  8.61 us

profile of v5, /device:TPU:39, one launch (start us, length us, event | category | flops | bytes accessed | tf_op | source)
XLA Modules:
  0.0 109.7 jit_solution(425374198340977764)
XLA Ops:
  0.6 0.0 copy-start.4
  0.6 0.0 copy-start.3
  0.7 30.4 %front.1 = (bf16[8,256,1024]{2,1,0:T(8,128)(2,1)}, bf16[2048,128]{1,0:T(8,128)(2,1)S(1)}, bf16[2048,128]{1,0:T(8,128)(2,1)S(1)}, bf16[4096,256]{1,0:T(8,128)(2,1...) custom-call(bf16[256,1024]{1,0:T(8,128)(2,1)} %tok_ref.3, bf16[256,1024]{1,0:T(8,128)(2,1)} %go_ref.3, ...), custom_call_target="tpu_custom_call" | custom-call | tf_op jit(solution)/shard_map/front/pallas_call | solution.py:388
  31.0 0.0 copy-start.2
  31.0 0.0 copy-done.4
  31.1 0.0 copy-done.3
  31.1 6.3 %attn_fwd.1 = (f32[2048,128]{1,0:T(8,128)S(1)}, f32[2,16,128]{2,1,0:T(8,128)S(1)}) custom-call(s32[64]{0:T(128)S(1)} %copy-done.3, s32[64]{0:T(128)S(1)} %copy-done.4, bf16[2048,128]{1,0:T(8,128)(2,1)S(1)} %get-tuple-element.19.q_ref, bf16[4096,256]{1,0:T(8,128)(2,1)S(1)} %get-tuple-element.20.kv_ref, bf16[2048,128]{1,0:T(8,128)(2,1)S(1)} %get-tuple-element.21.u_ref, ...), custom_call_target="tpu_custom_call" | custom-call | flops 1000000000 | bytes 4194304 | tf_op jit(solution)/shard_map/attn_fwd/pallas_call | solution.py:645
  37.4 8.6 %stats.1.stat_ref = f32[2,16,128]{2,1,0:T(8,128)S(1)} custom-call(f32[2,16,128]{2,1,0:T(8,128)S(1)} %get-tuple-element.24.s_ref), custom_call_target="tpu_custom_call" | custom-call | tf_op jit(solution)/shard_map/stats/pallas_call | solution.py:424
  46.0 0.0 copy-start
  46.0 0.0 copy-start.1
  46.0 9.8 %attn_bwd.1 = (bf16[2048,128]{1,0:T(8,128)(2,1)S(1)}, bf16[2048,128]{1,0:T(8,128)(2,1)S(1)}, bf16[2048,128]{1,0:T(8,128)(2,1)S(1)}, f32[2048,256]{1,0:T(8,128)S(1)}, bf16[2048,256]{1,0:T(8,128)(2,1)S(1)}) custom-call(s32[64]{0:T(128)S(1)} %copy-done.3, s32[64]{0:T(128)S(1)} %copy-done.4, bf16[2048,128]{1,0:T(8,128)(2,1)S(1)} %get-tuple-element.19.q_ref, ...), custom_call_target="tpu_custom_call" | custom-call | flops 2000000000 | bytes 4194304 | tf_op jit(solution)/shard_map/attn_bwd/pallas_call | solution.py:645
  55.9 0.0 copy-done.2
  55.9 0.0 copy-done
  55.9 0.0 copy-done.1
  55.9 52.6 %back.1 = (bf16[256,1024]{1,0:T(8,128)(2,1)S(1)}, bf16[256,1024]{1,0:T(8,128)(2,1)S(1)}, f32[32,1024]{1,0:T(8,128)S(1)}) custom-call(bf16[256,1024]{1,0:T(8,128)(2,1)S(1)} %copy-done, bf16[256,1024]{1,0:T(8,128)(2,1)S(1)} %copy-done.1, bf16[2048,128]{1,0:T(8,128)(2,1)S(1)} %get-tuple-element.26.gated_ref, bf16[2048,128]{1,0:T(8,128)(2,1)S(1)} %get-tuple-element.27.du_ref, ...), custom_call_target="tpu_custom_call" | custom-call | tf_op jit(solution)/shard_map/back/pallas_call | solution.py:603
  108.5 1.0 store.1
Async XLA Ops:
  0.6 30.4 %copy-start.4 = (s32[64]{0:T(128)S(1)}, s32[64]{0:T(128)}, u32[]{:S(2)}) copy-start(s32[64]{0:T(128)} %tails_ref.3) | copy-start | bytes 772
  0.6 30.4 %copy-start.3 = (s32[64]{0:T(128)S(1)}, s32[64]{0:T(128)}, u32[]{:S(2)}) copy-start(s32[64]{0:T(128)} %counts_ref.3) | copy-start | bytes 772
  31.0 24.8 %copy-start.2 = (bf16[2048,512]{1,0:T(8,128)(2,1)}, bf16[2048,512]{1,0:T(8,128)(2,1)S(1)}, u32[]{:S(2)}) copy-start(bf16[2048,512]{1,0:T(8,128)(2,1)S(1)} %get-tuple-element.25.slope_ref) | copy-start | bytes 6291460
  46.0 9.9 %copy-start = (bf16[256,1024]{1,0:T(8,128)(2,1)S(1)}, bf16[256,1024]{1,0:T(8,128)(2,1)}, u32[]{:S(2)}) copy-start(bf16[256,1024]{1,0:T(8,128)(2,1)} %tok_ref.3) | copy-start | bytes 1572868
  46.0 9.9 %copy-start.1 = (bf16[256,1024]{1,0:T(8,128)(2,1)S(1)}, bf16[256,1024]{1,0:T(8,128)(2,1)}, u32[]{:S(2)}) copy-start(bf16[256,1024]{1,0:T(8,128)(2,1)} %go_ref.3) | copy-start | bytes 1572868

commit v6 on v5

--- a/solution.py
+++ b/solution.py
@@ -440,7 +440,9 @@
     groups, piece = held.shape[1] + 1, held.shape[2]
     rows = tok_ref.shape[0]
     peers = group_peers(me, pos)
-    plane = [lax.rem(group + step, groups) * HEADS + pos for step in range(1, groups)]
+    steps = sorted(((dz, dx) for dz in range(4) for dx in range(4) if dz or dx), key=lambda s: -min(s[0], 4 - s[0]) - min(s[1], 4 - s[1]))
+    plane_groups = [lax.rem(group // 4 + dz, 4) * 4 + lax.rem(lax.rem(group, 4) + dx, 4) for dz, dx in steps]
+    plane = [to * HEADS + pos for to in plane_groups]
     after, before = lax.rem(me + HEADS, n), lax.rem(me + n - HEADS, n)
     has_before, has_after = group > 0, group < groups - 1
     dests = [(2 * (group // 8) + r) * 32 + pos * 4 + lax.rem(group, 8) // 2 for r in range(2)]
@@ -509,8 +511,7 @@
 
     def scatter(r):
         for i, peer in enumerate(plane):
-            to = lax.rem(group + i + 1, groups)
-            scattered.append(send(parts.at[r, share(to, piece)], held.at[r, i], w_s.at[r, i], w_r.at[r, i], peer))
+            scattered.append(send(parts.at[r, share(plane_groups[i], piece)], held.at[r, i], w_s.at[r, i], w_r.at[r, i], peer))
 
     def collect(r):
         acc = parts[r, share(group, piece), :].astype(jnp.float32)
@@ -536,7 +537,6 @@
     loads[2].start()
     grad = dot(jnp.concatenate([du_ref[...], dq_ref[...]], axis=1), xs[...], TN)
     fill(0, [grad[:HD], grad[HD:]])
-    scatter(0)
     late = []
     for i, to in enumerate(turn):
         for needed, copy in halo[2 * i : 2 * i + 2]:
@@ -552,6 +552,8 @@
                 late.append(send(d_kv.at[here, cols], dst, late_s.at[j, i], late_r.at[j, i], peers[i]))
             else:
                 d_full[:, columns(b)] = val
+        if i == 5:
+            scatter(0)
         grad = dot(d_kv[here, :], xs[here, :], TN)
         if i < HEADS - 1:
             grads[...] = grad if i == 0 else grads[...] + grad

time: 110 us -> 111 us (level)
    pallas_call x2, Pallas kernels: 16.1 us -> 19.6 us  [attention_call(): pl.pallas_call(kernel, grid_spec=pltpu.PrefetchScalarGridSpec(num_scalar_...]
    pallas_call x1, Pallas kernels: 52.6 us -> 50.7 us  [back(): pl.pallas_call(back_kernel, out_shape=[shape((rows, D), bf), shape((rows,...]
where the time goes in v6:
time: 111 us
  Pallas kernels  110 us (99%)
    pallas_call x1, Pallas kernels, back(): pl.pallas_call(back_kernel, out_shape=[shape((rows, D), bf), shape((rows,...  50.7 us
    pallas_call x1, Pallas kernels, front(): pl.pallas_call(front_kernel, out_shape=[shape(HEADS, rows, D), shape(span...  30.4 us
    pallas_call x2, Pallas kernels, attention_call(): pl.pallas_call(kernel, grid_spec=pltpu.PrefetchScalarGridSpec(num_scalar_...  19.6 us
    pallas_call x1, Pallas kernels, sum_stats(): pl.pallas_call(stats_kernel, out_shape=jax.ShapeDtypeStruct(stats.shape,...  8.61 us

profile of v6, /device:TPU:39, one launch (start us, length us, event | category | flops | bytes accessed | tf_op | source)
XLA Modules:
  0.0 111.3 jit_solution(2032169653876972470)
XLA Ops:
  0.6 0.0 copy-start.4
  0.6 0.0 copy-start.3
  0.7 30.4 %front.1 = (bf16[8,256,1024]{2,1,0:T(8,128)(2,1)}, bf16[2048,128]{1,0:T(8,128)(2,1)S(1)}, bf16[2048,128]{1,0:T(8,128)(2,1)S(1)}, bf16[4096,256]{1,0:T(8,128)(2,1...) custom-call(bf16[256,1024]{1,0:T(8,128)(2,1)} %tok_ref.3, bf16[256,1024]{1,0:T(8,128)(2,1)} %go_ref.3, ...), custom_call_target="tpu_custom_call" | custom-call | tf_op jit(solution)/shard_map/front/pallas_call | solution.py:388
  31.0 0.0 copy-start.2
  31.0 0.0 copy-done.4
  31.1 0.0 copy-done.3
  31.1 7.4 %attn_fwd.1 = (f32[2048,128]{1,0:T(8,128)S(1)}, f32[2,16,128]{2,1,0:T(8,128)S(1)}) custom-call(s32[64]{0:T(128)S(1)} %copy-done.3, s32[64]{0:T(128)S(1)} %copy-done.4, bf16[2048,128]{1,0:T(8,128)(2,1)S(1)} %get-tuple-element.19.q_ref, bf16[4096,256]{1,0:T(8,128)(2,1)S(1)} %get-tuple-element.20.kv_ref, bf16[2048,128]{1,0:T(8,128)(2,1)S(1)} %get-tuple-element.21.u_ref, ...), custom_call_target="tpu_custom_call" | custom-call | flops 1000000000 | bytes 4194304 | tf_op jit(solution)/shard_map/attn_fwd/pallas_call | solution.py:647
  38.4 8.6 %stats.1.stat_ref = f32[2,16,128]{2,1,0:T(8,128)S(1)} custom-call(f32[2,16,128]{2,1,0:T(8,128)S(1)} %get-tuple-element.24.s_ref), custom_call_target="tpu_custom_call" | custom-call | tf_op jit(solution)/shard_map/stats/pallas_call | solution.py:424
  47.1 0.0 copy-start
  47.1 0.0 copy-start.1
  47.1 12.2 %attn_bwd.1 = (bf16[2048,128]{1,0:T(8,128)(2,1)S(1)}, bf16[2048,128]{1,0:T(8,128)(2,1)S(1)}, bf16[2048,128]{1,0:T(8,128)(2,1)S(1)}, f32[2048,256]{1,0:T(8,128)S(1)}, bf16[2048,256]{1,0:T(8,128)(2,1)S(1)}) custom-call(s32[64]{0:T(128)S(1)} %copy-done.3, s32[64]{0:T(128)S(1)} %copy-done.4, bf16[2048,128]{1,0:T(8,128)(2,1)S(1)} %get-tuple-element.19.q_ref, ...), custom_call_target="tpu_custom_call" | custom-call | flops 2000000000 | bytes 4194304 | tf_op jit(solution)/shard_map/attn_bwd/pallas_call | solution.py:647
  59.3 0.0 copy-done.2
  59.3 0.0 copy-done
  59.3 0.0 copy-done.1
  59.3 50.7 %back.1 = (bf16[256,1024]{1,0:T(8,128)(2,1)S(1)}, bf16[256,1024]{1,0:T(8,128)(2,1)S(1)}, f32[32,1024]{1,0:T(8,128)S(1)}) custom-call(bf16[256,1024]{1,0:T(8,128)(2,1)S(1)} %copy-done, bf16[256,1024]{1,0:T(8,128)(2,1)S(1)} %copy-done.1, bf16[2048,128]{1,0:T(8,128)(2,1)S(1)} %get-tuple-element.26.gated_ref, bf16[2048,128]{1,0:T(8,128)(2,1)S(1)} %get-tuple-element.27.du_ref, ...), custom_call_target="tpu_custom_call" | custom-call | tf_op jit(solution)/shard_map/back/pallas_call | solution.py:605
  110.0 1.0 store.1
Async XLA Ops:
  0.6 30.4 %copy-start.4 = (s32[64]{0:T(128)S(1)}, s32[64]{0:T(128)}, u32[]{:S(2)}) copy-start(s32[64]{0:T(128)} %tails_ref.3) | copy-start | bytes 772
  0.6 30.4 %copy-start.3 = (s32[64]{0:T(128)S(1)}, s32[64]{0:T(128)}, u32[]{:S(2)}) copy-start(s32[64]{0:T(128)} %counts_ref.3) | copy-start | bytes 772
  31.0 28.3 %copy-start.2 = (bf16[2048,512]{1,0:T(8,128)(2,1)}, bf16[2048,512]{1,0:T(8,128)(2,1)S(1)}, u32[]{:S(2)}) copy-start(bf16[2048,512]{1,0:T(8,128)(2,1)S(1)} %get-tuple-element.25.slope_ref) | copy-start | bytes 6291460
  47.1 12.3 %copy-start = (bf16[256,1024]{1,0:T(8,128)(2,1)S(1)}, bf16[256,1024]{1,0:T(8,128)(2,1)}, u32[]{:S(2)}) copy-start(bf16[256,1024]{1,0:T(8,128)(2,1)} %tok_ref.3) | copy-start | bytes 1572868
  47.1 12.2 %copy-start.1 = (bf16[256,1024]{1,0:T(8,128)(2,1)S(1)}, bf16[256,1024]{1,0:T(8,128)(2,1)}, u32[]{:S(2)}) copy-start(bf16[256,1024]{1,0:T(8,128)(2,1)} %go_ref.3) | copy-start | bytes 1572868

commit v7 on v6

--- a/solution.py
+++ b/solution.py
@@ -476,10 +476,9 @@
     turn = [lax.rem(pos + i + 1, HEADS) for i in range(HEADS)]
     halo = []
     for i, to in enumerate(turn):
-        for h in (0, 1):
-            part = pl.ds(pl.multiple_of(to * rows + h * BLK, BLK), BLK)
+        half = pl.ds(pl.multiple_of(to * rows + BLK, BLK), rows - BLK)
+        for h, (part, needed) in enumerate(((block(to), to > 0), (half, to == 0))):
             copy = remote(far_ref.at[part], near.at[part], halo_s.at[i, h], halo_r.at[i, h], before)
-            needed = to + h > 0
             pl.when(needed & has_before)(copy.start)
             halo.append((needed, copy))
     near[:BLK, :] = jnp.zeros((BLK, 2 * HD), jnp.bfloat16)

time: 111 us -> 110 us (level)
    pallas_call x2, Pallas kernels: 19.6 us -> 16.2 us  [attention_call(): pl.pallas_call(kernel, grid_spec=pltpu.PrefetchScalarGridSpec(num_scalar_...]
    pallas_call x1, Pallas kernels: 50.7 us -> 52.4 us  [back(): pl.pallas_call(back_kernel, out_shape=[shape((rows, D), bf), shape((rows,...]
where the time goes in v7:
time: 110 us
  Pallas kernels  109 us (99%)
    pallas_call x1, Pallas kernels, back(): pl.pallas_call(back_kernel, out_shape=[shape((rows, D), bf), shape((rows,...  52.4 us
    pallas_call x1, Pallas kernels, front(): pl.pallas_call(front_kernel, out_shape=[shape(HEADS, rows, D), shape(span...  30.4 us
    pallas_call x2, Pallas kernels, attention_call(): pl.pallas_call(kernel, grid_spec=pltpu.PrefetchScalarGridSpec(num_scalar_...  16.2 us
    pallas_call x1, Pallas kernels, sum_stats(): pl.pallas_call(stats_kernel, out_shape=jax.ShapeDtypeStruct(stats.shape,...  8.61 us

profile of v7, /device:TPU:39, one launch (start us, length us, event | category | flops | bytes accessed | tf_op | source)
XLA Modules:
  0.0 109.6 jit_solution(16347133102128770216)
XLA Ops:
  0.6 0.0 copy-start.4
  0.6 0.0 copy-start.3
  0.7 30.4 %front.1 = (bf16[8,256,1024]{2,1,0:T(8,128)(2,1)}, bf16[2048,128]{1,0:T(8,128)(2,1)S(1)}, bf16[2048,128]{1,0:T(8,128)(2,1)S(1)}, bf16[4096,256]{1,0:T(8,128)(2,1...) custom-call(bf16[256,1024]{1,0:T(8,128)(2,1)} %tok_ref.3, bf16[256,1024]{1,0:T(8,128)(2,1)} %go_ref.3, ...), custom_call_target="tpu_custom_call" | custom-call | tf_op jit(solution)/shard_map/front/pallas_call | solution.py:388
  31.0 0.0 copy-start.2
  31.0 0.0 copy-done.4
  31.1 0.0 copy-done.3
  31.1 6.3 %attn_fwd.1 = (f32[2048,128]{1,0:T(8,128)S(1)}, f32[2,16,128]{2,1,0:T(8,128)S(1)}) custom-call(s32[64]{0:T(128)S(1)} %copy-done.3, s32[64]{0:T(128)S(1)} %copy-done.4, bf16[2048,128]{1,0:T(8,128)(2,1)S(1)} %get-tuple-element.19.q_ref, bf16[4096,256]{1,0:T(8,128)(2,1)S(1)} %get-tuple-element.20.kv_ref, bf16[2048,128]{1,0:T(8,128)(2,1)S(1)} %get-tuple-element.21.u_ref, ...), custom_call_target="tpu_custom_call" | custom-call | flops 1000000000 | bytes 4194304 | tf_op jit(solution)/shard_map/attn_fwd/pallas_call | solution.py:646
  37.4 8.6 %stats.1.stat_ref = f32[2,16,128]{2,1,0:T(8,128)S(1)} custom-call(f32[2,16,128]{2,1,0:T(8,128)S(1)} %get-tuple-element.24.s_ref), custom_call_target="tpu_custom_call" | custom-call | tf_op jit(solution)/shard_map/stats/pallas_call | solution.py:424
  46.0 0.0 copy-start
  46.0 0.0 copy-start.1
  46.0 9.9 %attn_bwd.1 = (bf16[2048,128]{1,0:T(8,128)(2,1)S(1)}, bf16[2048,128]{1,0:T(8,128)(2,1)S(1)}, bf16[2048,128]{1,0:T(8,128)(2,1)S(1)}, f32[2048,256]{1,0:T(8,128)S(1)}, bf16[2048,256]{1,0:T(8,128)(2,1)S(1)}) custom-call(s32[64]{0:T(128)S(1)} %copy-done.3, s32[64]{0:T(128)S(1)} %copy-done.4, bf16[2048,128]{1,0:T(8,128)(2,1)S(1)} %get-tuple-element.19.q_ref, ...), custom_call_target="tpu_custom_call" | custom-call | flops 2000000000 | bytes 4194304 | tf_op jit(solution)/shard_map/attn_bwd/pallas_call | solution.py:646
  55.9 0.0 copy-done.2
  55.9 0.0 copy-done
  55.9 0.0 copy-done.1
  56.0 52.4 %back.1 = (bf16[256,1024]{1,0:T(8,128)(2,1)S(1)}, bf16[256,1024]{1,0:T(8,128)(2,1)S(1)}, f32[32,1024]{1,0:T(8,128)S(1)}) custom-call(bf16[256,1024]{1,0:T(8,128)(2,1)S(1)} %copy-done, bf16[256,1024]{1,0:T(8,128)(2,1)S(1)} %copy-done.1, bf16[2048,128]{1,0:T(8,128)(2,1)S(1)} %get-tuple-element.26.gated_ref, bf16[2048,128]{1,0:T(8,128)(2,1)S(1)} %get-tuple-element.27.du_ref, ...), custom_call_target="tpu_custom_call" | custom-call | tf_op jit(solution)/shard_map/back/pallas_call | solution.py:604
  108.4 1.0 store.1
Async XLA Ops:
  0.6 30.4 %copy-start.4 = (s32[64]{0:T(128)S(1)}, s32[64]{0:T(128)}, u32[]{:S(2)}) copy-start(s32[64]{0:T(128)} %tails_ref.3) | copy-start | bytes 772
  0.6 30.4 %copy-start.3 = (s32[64]{0:T(128)S(1)}, s32[64]{0:T(128)}, u32[]{:S(2)}) copy-start(s32[64]{0:T(128)} %counts_ref.3) | copy-start | bytes 772
  31.0 24.9 %copy-start.2 = (bf16[2048,512]{1,0:T(8,128)(2,1)}, bf16[2048,512]{1,0:T(8,128)(2,1)S(1)}, u32[]{:S(2)}) copy-start(bf16[2048,512]{1,0:T(8,128)(2,1)S(1)} %get-tuple-element.25.slope_ref) | copy-start | bytes 6291460
  46.0 9.9 %copy-start = (bf16[256,1024]{1,0:T(8,128)(2,1)S(1)}, bf16[256,1024]{1,0:T(8,128)(2,1)}, u32[]{:S(2)}) copy-start(bf16[256,1024]{1,0:T(8,128)(2,1)} %tok_ref.3) | copy-start | bytes 1572868
  46.0 9.9 %copy-start.1 = (bf16[256,1024]{1,0:T(8,128)(2,1)S(1)}, bf16[256,1024]{1,0:T(8,128)(2,1)}, u32[]{:S(2)}) copy-start(bf16[256,1024]{1,0:T(8,128)(2,1)} %go_ref.3) | copy-start | bytes 1572868

commit v8 on v6

--- a/solution.py
+++ b/solution.py
@@ -87,7 +87,7 @@
         keep = (c <= r) & (c >= key - start)
         return body(rows_at(start + k_low, k_high - k_low), slice(q_low, q_high), keep)
 
-    pairs = full // 2 if k_dim == 0 else 0
+    pairs = full // 2
 
     def pair(j, carry):
         return carry + body(rows_at(start - (j + 1) * 2 * WIDE, 2 * WIDE), slice(0, size), None)

time: 111 us -> 111 us (level); the launches traced: 111 us -> 110 us
    pallas_call x2, Pallas kernels: 19.6 us -> 15.3 us  [attention_call(): pl.pallas_call(kernel, grid_spec=pltpu.PrefetchScalarGridSpec(num_scalar_...]
    pallas_call x1, Pallas kernels: 50.7 us -> 53.3 us  [back(): pl.pallas_call(back_kernel, out_shape=[shape((rows, D), bf), shape((rows,...]
where the time goes in v8:
time: 111 us; the launch traced here: 110 us
  Pallas kernels  109 us (98%)
    pallas_call x1, Pallas kernels, back(): pl.pallas_call(back_kernel, out_shape=[shape((rows, D), bf), shape((rows,...  53.3 us
    pallas_call x1, Pallas kernels, front(): pl.pallas_call(front_kernel, out_shape=[shape(HEADS, rows, D), shape(span...  30.4 us
    pallas_call x2, Pallas kernels, attention_call(): pl.pallas_call(kernel, grid_spec=pltpu.PrefetchScalarGridSpec(num_scalar_...  15.3 us
    pallas_call x1, Pallas kernels, sum_stats(): pl.pallas_call(stats_kernel, out_shape=jax.ShapeDtypeStruct(stats.shape,...  8.6 us

profile of v8, /device:TPU:39, one launch (start us, length us, event | category | flops | bytes accessed | tf_op | source)
XLA Modules:
  0.0 109.5 jit_solution(10254387551635500946)
XLA Ops:
  0.6 0.0 copy-start.4
  0.6 0.0 copy-start.3
  0.7 30.4 %front.1 = (bf16[8,256,1024]{2,1,0:T(8,128)(2,1)}, bf16[2048,128]{1,0:T(8,128)(2,1)S(1)}, bf16[2048,128]{1,0:T(8,128)(2,1)S(1)}, bf16[4096,256]{1,0:T(8,128)(2,1...) custom-call(bf16[256,1024]{1,0:T(8,128)(2,1)} %tok_ref.3, bf16[256,1024]{1,0:T(8,128)(2,1)} %go_ref.3, ...), custom_call_target="tpu_custom_call" | custom-call | tf_op jit(solution)/shard_map/front/pallas_call | solution.py:388
  31.0 0.0 copy-start.2
  31.0 0.0 copy-done.4
  31.1 0.0 copy-done.3
  31.1 6.0 %attn_fwd.1 = (f32[2048,128]{1,0:T(8,128)S(1)}, f32[2,16,128]{2,1,0:T(8,128)S(1)}) custom-call(s32[64]{0:T(128)S(1)} %copy-done.3, s32[64]{0:T(128)S(1)} %copy-done.4, bf16[2048,128]{1,0:T(8,128)(2,1)S(1)} %get-tuple-element.19.q_ref, bf16[4096,256]{1,0:T(8,128)(2,1)S(1)} %get-tuple-element.20.kv_ref, bf16[2048,128]{1,0:T(8,128)(2,1)S(1)} %get-tuple-element.21.u_ref, ...), custom_call_target="tpu_custom_call" | custom-call | flops 1000000000 | bytes 4194304 | tf_op jit(solution)/shard_map/attn_fwd/pallas_call | solution.py:647
  37.1 8.6 %stats.1.stat_ref = f32[2,16,128]{2,1,0:T(8,128)S(1)} custom-call(f32[2,16,128]{2,1,0:T(8,128)S(1)} %get-tuple-element.24.s_ref), custom_call_target="tpu_custom_call" | custom-call | tf_op jit(solution)/shard_map/stats/pallas_call | solution.py:424
  45.7 0.0 copy-start
  45.7 0.0 copy-start.1
  45.7 9.3 %attn_bwd.1 = (bf16[2048,128]{1,0:T(8,128)(2,1)S(1)}, bf16[2048,128]{1,0:T(8,128)(2,1)S(1)}, bf16[2048,128]{1,0:T(8,128)(2,1)S(1)}, f32[2048,256]{1,0:T(8,128)S(1)}, bf16[2048,256]{1,0:T(8,128)(2,1)S(1)}) custom-call(s32[64]{0:T(128)S(1)} %copy-done.3, s32[64]{0:T(128)S(1)} %copy-done.4, bf16[2048,128]{1,0:T(8,128)(2,1)S(1)} %get-tuple-element.19.q_ref, ...), custom_call_target="tpu_custom_call" | custom-call | flops 2000000000 | bytes 4194304 | tf_op jit(solution)/shard_map/attn_bwd/pallas_call | solution.py:647
  55.0 0.0 copy-done.2
  55.0 0.0 copy-done
  55.0 0.0 copy-done.1
  55.0 53.3 %back.1 = (bf16[256,1024]{1,0:T(8,128)(2,1)S(1)}, bf16[256,1024]{1,0:T(8,128)(2,1)S(1)}, f32[32,1024]{1,0:T(8,128)S(1)}) custom-call(bf16[256,1024]{1,0:T(8,128)(2,1)S(1)} %copy-done, bf16[256,1024]{1,0:T(8,128)(2,1)S(1)} %copy-done.1, bf16[2048,128]{1,0:T(8,128)(2,1)S(1)} %get-tuple-element.26.gated_ref, bf16[2048,128]{1,0:T(8,128)(2,1)S(1)} %get-tuple-element.27.du_ref, ...), custom_call_target="tpu_custom_call" | custom-call | tf_op jit(solution)/shard_map/back/pallas_call | solution.py:605
  108.3 1.0 store.1
Async XLA Ops:
  0.6 30.4 %copy-start.4 = (s32[64]{0:T(128)S(1)}, s32[64]{0:T(128)}, u32[]{:S(2)}) copy-start(s32[64]{0:T(128)} %tails_ref.3) | copy-start | bytes 772
  0.6 30.4 %copy-start.3 = (s32[64]{0:T(128)S(1)}, s32[64]{0:T(128)}, u32[]{:S(2)}) copy-start(s32[64]{0:T(128)} %counts_ref.3) | copy-start | bytes 772
  31.0 23.9 %copy-start.2 = (bf16[2048,512]{1,0:T(8,128)(2,1)}, bf16[2048,512]{1,0:T(8,128)(2,1)S(1)}, u32[]{:S(2)}) copy-start(bf16[2048,512]{1,0:T(8,128)(2,1)S(1)} %get-tuple-element.25.slope_ref) | copy-start | bytes 6291460
  45.7 9.3 %copy-start = (bf16[256,1024]{1,0:T(8,128)(2,1)S(1)}, bf16[256,1024]{1,0:T(8,128)(2,1)}, u32[]{:S(2)}) copy-start(bf16[256,1024]{1,0:T(8,128)(2,1)} %tok_ref.3) | copy-start | bytes 1572868
  45.7 9.3 %copy-start.1 = (bf16[256,1024]{1,0:T(8,128)(2,1)S(1)}, bf16[256,1024]{1,0:T(8,128)(2,1)}, u32[]{:S(2)}) copy-start(bf16[256,1024]{1,0:T(8,128)(2,1)} %go_ref.3) | copy-start | bytes 1572868
